TPU v7x, 32 devices: a whole 2x2x4 slice. The times are simulated.
32 devices in a mesh: dp: 4 (over x, core), section: 2 (over y), tensor: 4 (over z).
Axes of the slice: x: 2, y: 2, z: 4, core: 2. Of those that a mesh axis runs over, the one named last changes fastest.
Arguments:
- arrivals: bfloat16 [2, 4, 128, 4096], P('section', 'dp', None, 'tensor'), may hold values from -30 to 30
- fresh: bfloat16 [2, 4, 128, 4096], P(None, 'dp', None, 'tensor'), may hold values from -30 to 30
- stash: bfloat16 [2, 2, 4, 128, 4096], P(None, 'section', 'dp', None, 'tensor'), may hold values from -30 to 30
- returning: bfloat16 [2, 4, 128, 4096], P('section', 'dp', None, 'tensor'), may hold values from -6 to 6
- loss_grad: bfloat16 [2, 4, 128, 4096], P(None, 'dp', None, 'tensor'), may hold values from -6 to 6
- gain: float32 [2, 4096], P('section', 'tensor'), may hold values from 0.1 to 1.9
- query_weight: bfloat16 [2, 4096, 4096], P('section', 'dp', 'tensor'), may hold values from -0.09375 to 0.09375
- key_weight: bfloat16 [2, 4096, 1024], P('section', 'dp', 'tensor'), may hold values from -0.09375 to 0.09375
- value_weight: bfloat16 [2, 4096, 1024], P('section', 'dp', 'tensor'), may hold values from -0.09375 to 0.09375
- w_out: bfloat16 [2, 4096, 4096], P('section', 'dp', 'tensor'), may hold values from -0.09375 to 0.09375
- plan: int32 [2, 4], replicated, may hold values from 0 to 3, each once within a row
- fresh_docs: int32 [2, 4, 128], replicated, may hold values from 0 to 5, never falling along the last dimension, each value on 1 to 64 neighbouring positions
- arrival_docs: int32 [2, 4, 128], P(None, 'dp'), may hold values from 0 to 5, never falling along the last dimension, each value on 1 to 64 neighbouring positions
- stash_docs: int32 [2, 2, 4, 128], P(None, 'section', 'dp'), may hold values from 0 to 5, never falling along the last dimension, each value on 1 to 64 neighbouring positions
Outputs:
- sent_forward: bfloat16 [2, 4, 128, 4096], P('section', 'dp', None, 'tensor')
- sent_backward: bfloat16 [2, 4, 128, 4096], P('section', 'dp', None, 'tensor')
- gain_grad: float32 [2, 4096], P('section', 'tensor')
Inputs may be any that keep to these rules, and one draw needn't show every extreme that they name: Each row of plan names every packed row of its micro-batch once. `fresh_docs`: along a packed row document numbers never fall; every document holds 1 to 64 tokens and one holds exactly 64. `arrival_docs`: along a packed row document numbers never fall; every document holds 1 to 64 tokens and one holds exactly 64. `stash_docs`: along a packed row document numbers never fall; every document holds 1 to 64 tokens and one holds exactly 64.
All inputs are finite; a program needn't handle non-finite values.
Results may differ from a plain program's by a relative error of at most 0.035.
Values may be sent and summed in bfloat16 or wider, within the bound.
No kernel may reach another device: no remote copies, remote signals or barrier semaphores. Data moves between devices by JAX's collectives and lax.ppermute only.
A program may use at most 64 MiB of HBM per device.

v0:
```python
import math

import jax
import jax.numpy as jnp
from jax import lax
from jax.sharding import PartitionSpec as P

MODEL_WIDTH = 4096
QUERY_HEADS = 32
KEY_VALUE_HEADS = 8
HEAD_SIZE = 128
TICKS = 2


norm_eps = 1e-05


def partner_2(block, axis, bit):
    count = lax.axis_size(axis)
    route = []
    for low in range(count):
        high = low | 1 << bit
        if high != low and high < count:
            route += [(low, high), (high, low)]
    return lax.ppermute(block, axis, route)


def from_behind(value, axis, steps):
    count = lax.axis_size(axis)
    leading, last = (max(0, -steps), min(count, count - steps))
    return lax.ppermute(value, axis, [(source, source + steps) for source in range(leading, last)])


def document_mask(documents):
    length = documents.shape[-1]
    same = documents[:, :, None] == documents[:, None, :]
    causal = jnp.arange(length)[:, None] >= jnp.arange(length)[None, :]
    return jnp.logical_and(same, causal[None])[:, None, None]


def attention_probs(query_rows, key_rows, value_rows, documents, kv_heads):
    rows, length = documents.shape
    per_key = query_rows.shape[1] // (kv_heads * HEAD_SIZE)
    query_heads = query_rows.reshape(rows, length, kv_heads, per_key, HEAD_SIZE)
    heads_of_key = key_rows.reshape(rows, length, kv_heads, HEAD_SIZE)
    heads_of_value = value_rows.reshape(rows, length, kv_heads, HEAD_SIZE)
    scores = jnp.einsum(
        "rikgd,rjkd->rkgij", query_heads, heads_of_key, preferred_element_type=jnp.float32
    ) * HEAD_SIZE ** (-0.5)
    raised = jnp.where(document_mask(documents), jnp.exp(scores), 0.0)
    probs = raised / jnp.sum(raised, axis=-1, keepdims=True)
    return (query_heads, heads_of_key, heads_of_value, probs, probs.astype(jnp.bfloat16))


def local(
    arrivals,
    fresh,
    stash,
    returning,
    loss_grad,
    gain,
    query_weight,
    key_weight,
    value_weight,
    w_out,
    plan,
    fresh_docs,
    arrival_docs,
    stash_docs,
):
    tensor_count = lax.axis_size("tensor")
    section_count = lax.axis_size("section")
    replicas = lax.axis_size("dp")
    tensor_pos = lax.axis_index("tensor")
    section_pos = lax.axis_index("section")
    replica_pos = lax.axis_index("dp")
    rows, length, width = (arrivals.shape[1], arrivals.shape[2], arrivals.shape[3])
    tokens = rows * length
    heads_here = QUERY_HEADS // tensor_count
    group_width = QUERY_HEADS // KEY_VALUE_HEADS
    share_count = max(1, group_width // heads_here)
    bit_count = share_count.bit_length() - 1
    query_cols = heads_here * HEAD_SIZE
    query_w, key_w, value_w, out_w = (
        lax.all_gather(query_weight[0], "dp", axis=0, tiled=True),
        lax.all_gather(key_weight[0], "dp", axis=0, tiled=True),
        lax.all_gather(value_weight[0], "dp", axis=0, tiled=True),
        lax.all_gather(w_out[0], "dp", axis=0, tiled=True),
    )
    grad_weights = jnp.concatenate([query_w, key_w, value_w], axis=1)
    paired = jnp.stack([key_w, value_w])
    for bit_pos in range(bit_count):
        partner = partner_2(paired, "tensor", bit_pos)
        low_side = tensor_pos >> bit_pos & 1 == 0
        paired = jnp.where(
            low_side, jnp.concatenate([paired, partner], -1), jnp.concatenate([partner, paired], -1)
        )
    forward_weights = jnp.concatenate([query_w, paired[0], paired[1]], axis=1)
    key_columns = (forward_weights.shape[1] - query_cols) // 2
    gathered = lax.all_gather(fresh, "dp", axis=1, tiled=True)
    sources = lax.dynamic_slice_in_dim(plan, replica_pos * rows, rows, 1)
    fresh_rows = jnp.stack(
        [jnp.take(gathered[tick], sources[tick], axis=0) for tick in range(TICKS)]
    )
    fresh_documents = jnp.stack(
        [jnp.take(fresh_docs[tick], sources[tick], axis=0) for tick in range(TICKS)]
    )
    gain_row = gain[0]
    outgoing = arrivals[0]
    going_back = returning[0]
    gain_total = jnp.zeros((width,), jnp.float32)
    for tick in range(TICKS):
        incoming = from_behind(outgoing, "section", 1)
        forward_in = jnp.where(section_pos == 0, fresh_rows[tick], incoming).reshape(tokens, width)
        from_arrivals = lax.dynamic_index_in_dim(
            arrival_docs, jnp.clip(section_pos - tick - 1, 0, section_count - 1), 0, keepdims=False
        )
        from_fresh = lax.dynamic_index_in_dim(
            fresh_documents, jnp.clip(tick - section_pos, 0, TICKS - 1), 0, keepdims=False
        )
        forward_docs = jnp.where(section_pos > tick, from_arrivals, from_fresh)
        arriving = from_behind(going_back, "section", -1)
        grad_in = jnp.where(section_pos == section_count - 1, loss_grad[tick], arriving).reshape(
            tokens, width
        )
        backward_in = stash[tick, 0].reshape(tokens, width)
        backward_docs = stash_docs[tick, 0]
        forward_f = forward_in.astype(jnp.float32)
        backward_f = backward_in.astype(jnp.float32)
        forward_sq, backward_sq = lax.psum(
            (jnp.sum(forward_f * forward_f, -1), jnp.sum(backward_f * backward_f, -1)), "tensor"
        )
        forward_inv = lax.rsqrt(forward_sq / MODEL_WIDTH + norm_eps)
        backward_inv = lax.rsqrt(backward_sq / MODEL_WIDTH + norm_eps)
        forward_normed = (forward_f * forward_inv[:, None] * gain_row).astype(jnp.bfloat16)
        backward_normed = (backward_f * backward_inv[:, None] * gain_row).astype(jnp.bfloat16)
        forward_proj = jnp.dot(
            lax.all_gather(forward_normed, "tensor", axis=1, tiled=True),
            forward_weights,
            preferred_element_type=jnp.float32,
        )
        backward_proj = jnp.dot(
            lax.all_gather(backward_normed, "tensor", axis=1, tiled=True),
            forward_weights,
            preferred_element_type=jnp.float32,
        )
        forward_proj = forward_proj.astype(jnp.bfloat16)
        backward_proj = backward_proj.astype(jnp.bfloat16)
        forward_query = forward_proj[:, :query_cols]
        forward_key = forward_proj[:, query_cols : query_cols + key_columns]
        forward_value = forward_proj[:, query_cols + key_columns :]
        backward_query = backward_proj[:, :query_cols]
        backward_key = backward_proj[:, query_cols : query_cols + key_columns]
        backward_value = backward_proj[:, query_cols + key_columns :]
        kv_heads = forward_key.shape[1] // HEAD_SIZE
        fwd_parts = attention_probs(
            forward_query, forward_key, forward_value, forward_docs, kv_heads
        )
        mixed = jnp.einsum(
            "rkgij,rjkd->rikgd", fwd_parts[4], fwd_parts[2], preferred_element_type=jnp.float32
        )
        mixed = mixed.astype(jnp.bfloat16).reshape(tokens, query_cols)
        attended = jnp.dot(
            lax.all_gather(mixed, "tensor", axis=1, tiled=True),
            out_w,
            preferred_element_type=jnp.float32,
        )
        outgoing = (forward_f + attended).astype(jnp.bfloat16).reshape(rows, length, width)
        query_heads, heads_of_key, heads_of_value, probs, probs_half = attention_probs(
            backward_query, backward_key, backward_value, backward_docs, kv_heads
        )
        head_gradient = lax.psum_scatter(
            lax.dot_general(
                out_w, grad_in, (((1,), (1,)), ((), ())), preferred_element_type=jnp.float32
            ).astype(jnp.bfloat16),
            "tensor",
            scatter_dimension=0,
            tiled=True,
        ).astype(jnp.float32)
        head_gradient = head_gradient.T.astype(jnp.bfloat16).reshape(query_heads.shape)
        prob_grad = jnp.einsum(
            "rikgd,rjkd->rkgij", head_gradient, heads_of_value, preferred_element_type=jnp.float32
        )
        score_grad = (
            probs
            * (prob_grad - jnp.sum(probs * prob_grad, axis=-1, keepdims=True))
            * HEAD_SIZE ** (-0.5)
        ).astype(jnp.bfloat16)
        query_grad = jnp.einsum(
            "rkgij,rjkd->rikgd", score_grad, heads_of_key, preferred_element_type=jnp.float32
        )
        query_grad = query_grad.astype(jnp.bfloat16).reshape(tokens, query_cols)
        key_grad = jnp.einsum(
            "rkgij,rikgd->rjkd", score_grad, query_heads, preferred_element_type=jnp.float32
        ).reshape(tokens, -1)
        value_grad = jnp.einsum(
            "rkgij,rikgd->rjkd", probs_half, head_gradient, preferred_element_type=jnp.float32
        ).reshape(tokens, -1)
        kv_grad = jnp.stack([key_grad, value_grad])
        for bit_pos in reversed(range(bit_count)):
            half = kv_grad.shape[-1] // 2
            low_side = tensor_pos >> bit_pos & 1 == 0
            keep = jnp.where(low_side, kv_grad[..., :half], kv_grad[..., half:])
            outward = jnp.where(low_side, kv_grad[..., half:], kv_grad[..., :half])
            kv_grad = keep + partner_2(outward.astype(jnp.bfloat16), "tensor", bit_pos).astype(
                outward.dtype
            )
        kv_grad = kv_grad.astype(jnp.bfloat16)
        grad_rows = jnp.concatenate([query_grad, kv_grad[0], kv_grad[1]], axis=1)
        normed_grad = (
            lax.psum_scatter(
                lax.dot_general(
                    grad_weights,
                    grad_rows,
                    (((1,), (1,)), ((), ())),
                    preferred_element_type=jnp.float32,
                ).astype(jnp.bfloat16),
                "tensor",
                scatter_dimension=0,
                tiled=True,
            )
            .astype(jnp.float32)
            .T
        )
        scaled = normed_grad * gain_row
        row_dot = lax.psum(jnp.sum(scaled * backward_f, -1), "tensor")
        result = (
            grad_in.astype(jnp.float32)
            + backward_inv[:, None] * scaled
            - backward_f * (backward_inv**3 * row_dot / MODEL_WIDTH)[:, None]
        )
        going_back = result.astype(jnp.bfloat16).reshape(rows, length, width)
        gain_total = gain_total + jnp.sum(normed_grad * backward_f * backward_inv[:, None], axis=0)
    gain_grad = lax.psum(gain_total, "dp") / math.sqrt(TICKS * rows * replicas * length)
    return (outgoing[None], going_back[None], gain_grad[None])


def solution(mesh):
    return jax.shard_map(
        local,
        mesh=mesh,
        in_specs=(
            P("section", "dp", None, "tensor"),
            P(None, "dp", None, "tensor"),
            P(None, "section", "dp", None, "tensor"),
            P("section", "dp", None, "tensor"),
            P(None, "dp", None, "tensor"),
            P("section", "tensor"),
            P("section", "dp", "tensor"),
            P("section", "dp", "tensor"),
            P("section", "dp", "tensor"),
            P("section", "dp", "tensor"),
            P(),
            P(),
            P(None, "dp", None),
            P(None, "section", "dp", None),
        ),
        out_specs=(
            P("section", "dp", None, "tensor"),
            P("section", "dp", None, "tensor"),
            P("section", "tensor"),
        ),
        check_vma=False,
    )
```

profile of v0, /device:TPU:0, one launch (start us, length us, event | category | flops | bytes accessed | tf_op | source)
XLA Modules:
  0.0 572.5 jit_solution(11700882372928945518)
XLA Ops:
  9.1 13.5 %psum.51 = f32[128]{0:T(128)S(1)} all-reduce(f32[128]{0:T(128)S(1)} %fusion.60), channel_id=1, replica_groups=mesh['dp'=4,'section'=2,'tensor'=4] {'tensor'}, use_global_device_ids=true, to_apply=%region_7.10 | all-reduce | flops 128 | bytes 1024 | tf_op jit(solution)/shard_map/psum | solution.py:130
  34.9 35.7 %all-gather.36.cloned.1.call-done = bf16[1,4096,1024]{2,1,0:T(8,128)(2,1)} async-done(((bf16[1,1024,1024]{2,1,0:T(8,128)(2,1)}), bf16[1,4096,1024]{2,1,0:T(8,128)(2,1)}) %all-gather.36.cloned.1.call-update) | async-done | bytes 8388624 | tf_op jit(solution)/shard_map/all_gather | solution.py:88
  70.6 7.4 %fusion.17 = bf16[4096,128]{0,1:T(8,128)(2,1)} fusion(bf16[1,4096,1024]{2,1,0:T(8,128)(2,1)} %all-gather.36.cloned.1.call-done, bf16[1,128,1024]{2,1,0:T(8,128)(2,1)S(1)} %collective-permute-done.2, bf16[2,1,128,1024]{3,2,1,0:T(8,128)(2,1)} %param.22, pred[]{:T(512)S(6)} %eq.95), kind=kOutput, calls=%fused_computation.14 | convolution fusion | flops 1074397184 | bytes 9961473 | tf_op jit(solution)/shard_map/dot_general | solution.py:173
  79.0 21.8 %all-gather.26.cloned.1.call-done = bf16[128,4096]{1,0:T(8,128)(2,1)} async-done(((bf16[128,1024]{1,0:T(8,128)(2,1)}), bf16[128,4096]{1,0:T(8,128)(2,1)}) %all-gather.26.cloned.1.call-update) | async-done | bytes 1048592 | tf_op jit(solution)/shard_map/all_gather | solution.py:143
  100.7 23.7 %all-gather.34.cloned.1.call-done = bf16[1,4096,256]{2,1,0:T(8,128)(2,1)} async-done(((bf16[1,1024,256]{2,1,0:T(8,128)(2,1)}), bf16[1,4096,256]{2,1,0:T(8,128)(2,1)}) %all-gather.34.cloned.1.call-update) | async-done | bytes 2097168 | tf_op jit(solution)/shard_map/all_gather | solution.py:87
  124.4 24.0 %all-gather.32.cloned.1.call-done = bf16[1,4096,256]{2,1,0:T(8,128)(2,1)} async-done(((bf16[1,1024,256]{2,1,0:T(8,128)(2,1)}), bf16[1,4096,256]{2,1,0:T(8,128)(2,1)}) %all-gather.32.cloned.1.call-update) | async-done | bytes 2097168 | tf_op jit(solution)/shard_map/all_gather | solution.py:86
  148.4 59.7 %all-gather.30.cloned.1.call-done = bf16[1,4096,1024]{2,1,0:T(8,128)(2,1)} async-done(((bf16[1,1024,1024]{2,1,0:T(8,128)(2,1)}), bf16[1,4096,1024]{2,1,0:T(8,128)(2,1)}) %all-gather.30.cloned.1.call-update) | async-done | bytes 8388624 | tf_op jit(solution)/shard_map/all_gather | solution.py:85
  208.2 9.9 %convolution_convert_fusion.3 = bf16[128,1536]{1,0:T(8,128)(2,1)S(1)} fusion(bf16[128,4096]{1,0:T(8,128)(2,1)} %all-gather.26.cloned.1.call-done, bf16[4096,256]{1,0:T(8,128)(2,1)} %bitcast.342, bf16[4096,256]{1,0:T(8,128)(2,1)} %bitcast.348, bf16[4096,1024]{1,0:T(8,128)(2,1)} %bitcast.336), kind=kOutput, calls=%fused_computation.16 | convolution fusion | flops 1648558080 | bytes 14024704 | tf_op jit(solution)/shard_map/dot_general | solution.py:142
  218.8 18.7 %reduce-scatter.5.cloned.1.call-done = bf16[1024,128]{0,1:T(8,128)(2,1)} async-done(((bf16[4096,128]{0,1:T(8,128)(2,1)}), bf16[1024,128]{0,1:T(8,128)(2,1)}) %reduce-scatter.5.cloned.1.call-update) | async-done | bytes 262160 | tf_op jit(solution)/shard_map/reduce_scatter | solution.py:172
  239.7 12.0 %convolution_convert_fusion.1 = bf16[4096,128]{0,1:T(8,128)(2,1)} fusion(bf16[128,256]{0,1:T(8,128)(2,1)S(1)} %bitcast.357, bf16[128,256]{0,1:T(8,128)(2,1)S(1)} %bitcast.327, bf16[128,1024]{0,1:T(8,128)(2,1)S(1)} %bitcast.316, bf16[4096,256]{1,0:T(8,128)(2,1)} %bitcast.343, bf16[4096,256]{1,0:T(8,128)(2,1)} %bitcast.349, bf16[4096,1024]{1,0:T(8,128)(2,1)} %bitcast.337), kind=kOutput, calls=%fused_computation.10 | convolution fusion | flops 1650065408 | bytes 14024704 | tf_op jit(solution)/shard_map/dot_general | solution.py:212
  262.3 27.6 %reduce-scatter.7.cloned.1.call-done = bf16[1024,128]{0,1:T(8,128)(2,1)} async-done(((bf16[4096,128]{0,1:T(8,128)(2,1)}), bf16[1024,128]{0,1:T(8,128)(2,1)}) %reduce-scatter.7.cloned.1.call-update) | async-done | bytes 262160 | tf_op jit(solution)/shard_map/reduce_scatter | solution.py:211
  291.2 9.4 %all-reduce.1 = (f32[128]{0:T(128)S(1)}, f32[128]{0:T(128)S(1)}, f32[128]{0:T(128)S(1)}) all-reduce(f32[128]{0:T(128)S(1)} %get-tuple-element.39, f32[128]{0:T(128)S(1)} %get-tuple-element.30, f32[128]{0:T(128)S(1)} %get-tuple-element.31), channel_id=1, replica_groups=mesh['dp'=4,'section'=2,'tensor'=4] {'tensor'}, use_global_device_ids=true, to_apply=%region_1.3 | all-reduce | flops 384 | bytes 3072 | tf_op jit(solution)/shard_map/psum | solution.py:130
  318.2 11.0 %all-gather.28.cloned.1.call-done = bf16[128,4096]{1,0:T(8,128)(2,1)} async-done(((bf16[128,1024]{1,0:T(8,128)(2,1)}), bf16[128,4096]{1,0:T(8,128)(2,1)}) %all-gather.28.cloned.1.call-update) | async-done | bytes 1048592 | tf_op jit(solution)/shard_map/all_gather | solution.py:143
  329.2 9.9 %convolution_convert_fusion.2 = bf16[128,1536]{1,0:T(8,128)(2,1)S(1)} fusion(bf16[128,4096]{1,0:T(8,128)(2,1)} %all-gather.28.cloned.1.call-done, bf16[4096,256]{1,0:T(8,128)(2,1)} %bitcast.344, bf16[4096,256]{1,0:T(8,128)(2,1)} %bitcast.350, bf16[4096,1024]{1,0:T(8,128)(2,1)} %bitcast.338), kind=kOutput, calls=%fused_computation.15 | convolution fusion | flops 1648558080 | bytes 14024704 | tf_op jit(solution)/shard_map/dot_general | solution.py:142
  340.4 17.6 %reduce-scatter.9.cloned.1.call-done = bf16[1024,128]{0,1:T(8,128)(2,1)} async-done(((bf16[4096,128]{0,1:T(8,128)(2,1)}), bf16[1024,128]{0,1:T(8,128)(2,1)}) %reduce-scatter.9.cloned.1.call-update) | async-done | bytes 262160 | tf_op jit(solution)/shard_map/reduce_scatter | solution.py:172
  362.8 11.8 %convolution_convert_fusion = bf16[4096,128]{0,1:T(8,128)(2,1)} fusion(bf16[128,256]{0,1:T(8,128)(2,1)S(1)} %bitcast.356, bf16[128,256]{0,1:T(8,128)(2,1)S(1)} %bitcast.328, bf16[128,1024]{0,1:T(8,128)(2,1)S(1)} %bitcast.319, bf16[4096,256]{1,0:T(8,128)(2,1)} %bitcast.345, bf16[4096,256]{1,0:T(8,128)(2,1)} %bitcast.351, bf16[4096,1024]{1,0:T(8,128)(2,1)} %bitcast.339), kind=kOutput, calls=%fused_computation.9 | convolution fusion | flops 1650065408 | bytes 14024704 | tf_op jit(solution)/shard_map/dot_general | solution.py:212
  374.7 25.9 %reduce-scatter.11.cloned.1.call-done = bf16[1024,128]{0,1:T(8,128)(2,1)} async-done(((bf16[4096,128]{0,1:T(8,128)(2,1)}), bf16[1024,128]{0,1:T(8,128)(2,1)}) %reduce-scatter.11.cloned.1.call-update) | async-done | bytes 262160 | tf_op jit(solution)/shard_map/reduce_scatter | solution.py:211
  404.9 24.3 %all-gather.18.cloned.1.call-done = bf16[128,4096]{1,0:T(8,128)(2,1)} async-done(((bf16[128,1024]{1,0:T(8,128)(2,1)}), bf16[128,4096]{1,0:T(8,128)(2,1)}) %all-gather.18.cloned.1.call-update) | async-done | bytes 1048592 | tf_op jit(solution)/shard_map/all_gather | solution.py:138
  429.2 9.9 %convolution_convert_fusion.5 = bf16[128,1536]{1,0:T(8,128)(2,1)S(1)} fusion(bf16[128,4096]{1,0:T(8,128)(2,1)} %all-gather.18.cloned.1.call-done, bf16[4096,256]{1,0:T(8,128)(2,1)} %bitcast.346, bf16[4096,256]{1,0:T(8,128)(2,1)} %bitcast.352, bf16[4096,1024]{1,0:T(8,128)(2,1)} %bitcast.340), kind=kOutput, calls=%fused_computation.18 | convolution fusion | flops 1648558080 | bytes 14024704 | tf_op jit(solution)/shard_map/dot_general | solution.py:137
  440.8 27.5 %all-gather.20.cloned.1.call-done = bf16[128,4096]{0,1:T(8,128)(2,1)} async-done(((bf16[128,1024]{0,1:T(8,128)(2,1)}), bf16[128,4096]{0,1:T(8,128)(2,1)}) %all-gather.20.cloned.1.call-update) | async-done | bytes 1048592 | tf_op jit(solution)/shard_map/all_gather | solution.py:164
  482.3 10.6 %all-reduce = (f32[128]{0:T(128)S(1)}, f32[128]{0:T(128)S(1)}) all-reduce(f32[128]{0:T(128)S(1)} %get-tuple-element.37, f32[128]{0:T(128)S(1)} %get-tuple-element.28), channel_id=1, replica_groups=mesh['dp'=4,'section'=2,'tensor'=4] {'tensor'}, use_global_device_ids=true, to_apply=%region_4.7 | all-reduce | flops 256 | bytes 2048 | tf_op jit(solution)/shard_map/psum | solution.py:130
  494.0 27.2 %all-gather.22.cloned.1.call-done = bf16[128,4096]{1,0:T(8,128)(2,1)} async-done(((bf16[128,1024]{1,0:T(8,128)(2,1)}), bf16[128,4096]{1,0:T(8,128)(2,1)}) %all-gather.22.cloned.1.call-update) | async-done | bytes 1048592 | tf_op jit(solution)/shard_map/all_gather | solution.py:138
  521.2 9.9 %convolution_convert_fusion.4 = bf16[128,1536]{1,0:T(8,128)(2,1)S(1)} fusion(bf16[128,4096]{1,0:T(8,128)(2,1)} %all-gather.22.cloned.1.call-done, bf16[4096,256]{1,0:T(8,128)(2,1)} %bitcast.347, bf16[4096,256]{1,0:T(8,128)(2,1)} %bitcast.353, bf16[4096,1024]{1,0:T(8,128)(2,1)} %bitcast.341), kind=kOutput, calls=%fused_computation.17 | convolution fusion | flops 1648558080 | bytes 14024704 | tf_op jit(solution)/shard_map/dot_general | solution.py:137
  539.8 20.5 %all-gather.24.cloned.1.call-done = bf16[128,4096]{0,1:T(8,128)(2,1)} async-done(((bf16[128,1024]{0,1:T(8,128)(2,1)}), bf16[128,4096]{0,1:T(8,128)(2,1)}) %all-gather.24.cloned.1.call-update) | async-done | bytes 1048592 | tf_op jit(solution)/shard_map/all_gather | solution.py:164
  (127 shorter events, 84.8 us)
Async XLA Ops:
  7.2 248.0 %copy-start = (s32[2,4]{1,0:T(2,128)S(1)}, s32[2,4]{1,0:T(2,128)}, u32[]{:S(2)}) copy-start(s32[2,4]{1,0:T(2,128)} %param.28) | copy-start | bytes 100
  7.2 63.4 %all-gather.36.cloned.1.call-start = ((), (), s32[]{:S(2)}) async-start(), calls=%async_computation.18 | async-start | bytes 10485760 | tf_op jit(solution)/shard_map/all_gather | solution.py:88
  7.9 70.9 %copy-start.6 = (s32[2,1,1,128]{3,2,1,0:T(1,128)S(1)}, s32[2,1,1,128]{3,2,1,0:T(1,128)}, u32[]{:S(2)}) copy-start(s32[2,1,1,128]{3,2,1,0:T(1,128)} %param.31) | copy-start | bytes 3076
  7.9 92.8 %all-gather.26.cloned.1.call-start = ((), (), s32[]{:S(2)}) async-start(), calls=%async_computation.9 | async-start | bytes 1310720 | tf_op jit(solution)/shard_map/all_gather | solution.py:143
  24.4 99.9 %all-gather.34.cloned.1.call-start = ((), (), s32[]{:S(2)}) async-start(), calls=%async_computation.17 | async-start | bytes 2621440 | tf_op jit(solution)/shard_map/all_gather | solution.py:87
  25.2 123.2 %all-gather.32.cloned.1.call-start = ((), (), s32[]{:S(2)}) async-start(), calls=%async_computation.16 | async-start | bytes 2621440 | tf_op jit(solution)/shard_map/all_gather | solution.py:86
  25.8 182.4 %all-gather.30.cloned.1.call-start = ((), (), s32[]{:S(2)}) async-start(), calls=%async_computation.15 | async-start | bytes 10485760 | tf_op jit(solution)/shard_map/all_gather | solution.py:85
  26.3 211.1 %reduce-scatter.5.cloned.1.call-start = ((), (), s32[]{:S(2)}) async-start(), calls=%async_computation.10 | async-start | bytes 1310720 | tf_op jit(solution)/shard_map/reduce_scatter | solution.py:172
  26.4 8.5 %collective-permute-start.2 = (bf16[1,128,1024]{2,1,0:T(8,128)(2,1)}, bf16[1,128,1024]{2,1,0:T(8,128)(2,1)S(1)}, u32[]{:S(2)}, u32[]{:S(2)}) collective-permute-start(bf16[1,128,1024]{2,1,0:T(8,128)(2,1)} %bitcast.354), channel_id=1, source_target_pairs={{4,0},{5,1},{6,2},{7,3},{12,8},{13,9},{14,10},{15,11},{20,16},{21,... | collective-permute-start | bytes 786440 | tf_op jit(solution)/shard_map/ppermute | solution.py:31
  78.0 182.4 %all-gather.16.cloned.1.call-start = ((), (), s32[]{:S(2)}) async-start(), calls=%async_computation.4 | async-start | bytes 2621440 | tf_op jit(solution)/shard_map/all_gather | solution.py:100
  78.8 211.2 %reduce-scatter.7.cloned.1.call-start = ((), (), s32[]{:S(2)}) async-start(), calls=%async_computation.11 | async-start | bytes 1310720 | tf_op jit(solution)/shard_map/reduce_scatter | solution.py:211
  239.7 50.3 %copy-start.1 = (bf16[2,1,1,128,1024]{4,3,2,1,0:T(8,128)(2,1)S(1)}, bf16[2,1,1,128,1024]{4,3,2,1,0:T(8,128)(2,1)}, u32[]{:S(2)}) copy-start(bf16[2,1,1,128,1024]{4,3,2,1,0:T(8,128)(2,1)} %param.20) | copy-start | bytes 1572868
  239.7 60.9 %copy-start.2 = (bf16[2,1,128,1024]{3,2,1,0:T(8,128)(2,1)S(1)}, bf16[2,1,128,1024]{3,2,1,0:T(8,128)(2,1)}, u32[]{:S(2)}) copy-start(bf16[2,1,128,1024]{3,2,1,0:T(8,128)(2,1)} %param.22) | copy-start | bytes 1572868
  251.7 77.5 %all-gather.28.cloned.1.call-start = ((), (), s32[]{:S(2)}) async-start(), calls=%async_computation.12 | async-start | bytes 1310720 | tf_op jit(solution)/shard_map/all_gather | solution.py:143
  251.7 10.4 %collective-permute-start = (bf16[1,128,1024]{2,1,0:T(8,128)(2,1)S(1)}, bf16[1,128,1024]{2,1,0:T(8,128)(2,1)S(1)}, u32[]{:S(2)}, u32[]{:S(2)}) collective-permute-start(bf16[1,128,1024]{2,1,0:T(8,128)(2,1)S(1)} %bitcast.355), channel_id=1, source_target_pairs={{0,4},{1,5},{2,6},{3,7},{8,12},{9,13},{10,14},{11,15},{16,20},{17,... | collective-permute-start | bytes 786440 | tf_op jit(solution)/shard_map/ppermute | solution.py:31
  302.5 55.5 %reduce-scatter.9.cloned.1.call-start = ((), (), s32[]{:S(2)}) async-start(), calls=%async_computation.13 | async-start | bytes 1310720 | tf_op jit(solution)/shard_map/reduce_scatter | solution.py:172
  302.5 8.3 %collective-permute-start.3 = (bf16[1,128,1024]{2,1,0:T(8,128)(2,1)S(1)}, bf16[1,128,1024]{2,1,0:T(8,128)(2,1)S(1)}, u32[]{:S(2)}, u32[]{:S(2)}) collective-permute-start(bf16[1,128,1024]{2,1,0:T(8,128)(2,1)S(1)} %get-tuple-element.44), channel_id=1, source_target_pairs={{4,0},{5,1},{6,2},{7,3},{12,8},{13,9},{14,10},{15,11},{20,16},{21,... | collective-permute-start | bytes 786440 | tf_op jit(solution)/shard_map/ppermute | solution.py:31
  318.1 82.5 %reduce-scatter.11.cloned.1.call-start = ((), (), s32[]{:S(2)}) async-start(), calls=%async_computation.14 | async-start | bytes 1310720 | tf_op jit(solution)/shard_map/reduce_scatter | solution.py:211
  374.6 54.6 %all-gather.18.cloned.1.call-start = ((), (), s32[]{:S(2)}) async-start(), calls=%async_computation.5 | async-start | bytes 1310720 | tf_op jit(solution)/shard_map/all_gather | solution.py:138
  402.5 65.8 %all-gather.20.cloned.1.call-start = ((), (), s32[]{:S(2)}) async-start(), calls=%async_computation.6 | async-start | bytes 1310720 | tf_op jit(solution)/shard_map/all_gather | solution.py:164
  440.7 52.2 %copy-start.3 = (bf16[1024,128]{0,1:T(8,128)(2,1)S(1)}, bf16[1024,128]{0,1:T(8,128)(2,1)}, u32[]{:S(2)}) copy-start(bf16[1024,128]{0,1:T(8,128)(2,1)} %reduce-scatter.11.cloned.1.call-done) | copy-start | bytes 786436
  440.7 80.5 %all-gather.22.cloned.1.call-start = ((), (), s32[]{:S(2)}) async-start(), calls=%async_computation.7 | async-start | bytes 1310720 | tf_op jit(solution)/shard_map/all_gather | solution.py:138
  473.3 8.8 %collective-permute-start.1 = (bf16[1,128,1024]{2,1,0:T(8,128)(2,1)S(1)}, bf16[1,128,1024]{2,1,0:T(8,128)(2,1)S(1)}, u32[]{:S(2)}, u32[]{:S(2)}) collective-permute-start(bf16[1,128,1024]{2,1,0:T(8,128)(2,1)S(1)} %fusion.44), channel_id=1, source_target_pairs={{0,4},{1,5},{2,6},{3,7},{8,12},{9,13},{10,14},{11,15},{16,20},{17,... | collective-permute-start | bytes 786440 | tf_op jit(solution)/shard_map/ppermute | solution.py:31
  494.0 66.3 %all-gather.24.cloned.1.call-start = ((), (), s32[]{:S(2)}) async-start(), calls=%async_computation.8 | async-start | bytes 1310720 | tf_op jit(solution)/shard_map/all_gather | solution.py:164
  (4 other events, 146.4 us)
Sparse Core Ops, SparseCore 0:
  9.6 60.9 all-gather.35
  72.7 27.9 all-gather.25
  102.3 22.0 all-gather.33
  125.8 22.5 all-gather.31
  149.8 58.2 all-gather.29
  210.3 27.1 reduce-scatter.4
  239.1 21.2 all-gather.15
  262.8 27.1 reduce-scatter.6
  302.6 26.5 all-gather.27
  331.3 26.6 reduce-scatter.8
  374.8 25.7 reduce-scatter.10
  402.6 26.5 all-gather.17
  440.9 27.4 all-gather.19
  494.1 27.0 all-gather.21
  532.8 27.4 all-gather.23
where the time goes:
time: 573 us
  waiting for transfers between devices  391 us (68%)
  matrix products  95.6 us (17%)
  blocking collectives  39.8 us (7%)
  between operations  18.4 us (3%)
  other arithmetic  10.5 us (2%)
  starting transfers between devices  10.4 us (2%)
  local copies, waits for them, and re-layouts  7.32 us (1%)
    all_gather x1, waiting for transfers between devices, local(): lax.all_gather(query_weight[0], 'dp', axis=0, tiled=True)  59.7 us
    reduce_scatter x2, waiting for transfers between devices, local(): lax.psum_scatter(lax.dot_general(grad_weights, grad_rows, (((1,), (1,)),...  53.5 us
    all_gather x2, waiting for transfers between devices, local(): lax.all_gather(forward_normed, 'tensor', axis=1, tiled=True)  51.5 us
    all_gather x2, waiting for transfers between devices, local(): lax.all_gather(mixed, 'tensor', axis=1, tiled=True)  48.1 us
    reduce_scatter x2, waiting for transfers between devices, local(): lax.psum_scatter(lax.dot_general(out_w, grad_in, (((1,), (1,)), ((), ()))...  36.3 us
    all_gather x1, waiting for transfers between devices, local(): lax.all_gather(w_out[0], 'dp', axis=0, tiled=True)  35.7 us
    psum x3, blocking collectives, local(): lax.psum((jnp.sum(forward_f * forward_f, -1), jnp.sum(backward_f * backwa...  33.4 us
    all_gather x2, waiting for transfers between devices, local(): lax.all_gather(backward_normed, 'tensor', axis=1, tiled=True)  32.7 us
  transfers between devices with their start and end apart: 19, of which 18 were waited for; matrix products, arithmetic and copies ran while one was open for 10% of the time, Pallas kernels for 0%

commit v1 on v0

v1 whole, which is shorter than its diff:
```python
import math

import jax
import jax.numpy as jnp
from jax import lax
from jax.sharding import PartitionSpec as P

MODEL_WIDTH = 4096
QUERY_HEADS = 32
KEY_VALUE_HEADS = 8
HEAD_SIZE = 128
TICKS = 2
NORM_EPS = 1e-05
F32 = jnp.float32
BF16 = jnp.bfloat16


def exchange(block, axis, mask):
    count = lax.axis_size(axis)
    return lax.ppermute(block, axis, [(i, i ^ mask) for i in range(count)])


def shifted(value, axis, steps):
    count = lax.axis_size(axis)
    leading, last = (max(0, -steps), min(count, count - steps))
    return lax.ppermute(value, axis, [(source, source + steps) for source in range(leading, last)])


def document_mask(documents):
    length = documents.shape[-1]
    same = documents[:, None] == documents[None, :]
    causal = jnp.arange(length)[:, None] >= jnp.arange(length)[None, :]
    return jnp.logical_and(same, causal)[None, None]


def attention_probs(query_rows, key_rows, value_rows, documents, kv_heads):
    length = documents.shape[0]
    per_key = query_rows.shape[1] // (kv_heads * HEAD_SIZE)
    query_heads = query_rows.reshape(length, kv_heads, per_key, HEAD_SIZE)
    heads_of_key = key_rows.reshape(length, kv_heads, HEAD_SIZE)
    heads_of_value = value_rows.reshape(length, kv_heads, HEAD_SIZE)
    scores = jnp.einsum(
        "ikgd,jkd->kgij", query_heads, heads_of_key, preferred_element_type=F32
    ) * HEAD_SIZE ** (-0.5)
    raised = jnp.where(document_mask(documents), jnp.exp(scores), 0.0)
    probs = raised / jnp.sum(raised, axis=-1, keepdims=True)
    return (query_heads, heads_of_key, heads_of_value, probs, probs.astype(BF16))


def local(
    arrivals,
    fresh,
    stash,
    returning,
    loss_grad,
    gain,
    query_weight,
    key_weight,
    value_weight,
    w_out,
    plan,
    fresh_docs,
    arrival_docs,
    stash_docs,
):
    tensor_count = lax.axis_size("tensor")
    section_count = lax.axis_size("section")
    replicas = lax.axis_size("dp")
    tensor_pos = lax.axis_index("tensor")
    section_pos = lax.axis_index("section")
    replica_pos = lax.axis_index("dp")
    length, width = arrivals.shape[2:]
    heads_here = QUERY_HEADS // tensor_count
    group_width = QUERY_HEADS // KEY_VALUE_HEADS
    share_count = max(1, group_width // heads_here)
    bit_count = share_count.bit_length() - 1
    query_cols = heads_here * HEAD_SIZE
    key_cols = key_weight.shape[2]
    block_rows = query_weight.shape[1]
    relative = tensor_count == replicas
    shift = tensor_pos if relative else 0

    def gather_dp(weight):
        other = exchange(weight, "dp", 2)
        sibling = exchange(weight, "dp", 1)
        return [weight, sibling, other, exchange(other, "dp", 1)]

    def assemble(parts_list):
        cols = sum(parts[0].shape[1] for parts in parts_list)
        whole = jnp.zeros((block_rows * replicas, cols), BF16)
        for mask in range(replicas):
            row = (replica_pos ^ mask ^ shift) * block_rows
            col = 0
            for parts in parts_list:
                whole = lax.dynamic_update_slice(whole, parts[mask], (row, col))
                col += parts[mask].shape[1]
        return whole

    def gather(block):
        if not relative:
            return lax.all_gather(block, "tensor", axis=block.ndim - 1, tiled=True)
        return jnp.concatenate(
            [block] + [exchange(block, "tensor", mask) for mask in range(1, tensor_count)], -1
        )

    def product_scatter(left, right):
        contract = (((1,), (1,)), ((), ()))
        if not relative:
            part = lax.dot_general(right, left, contract, preferred_element_type=F32).astype(BF16)
            return lax.psum_scatter(part, "tensor", scatter_dimension=0, tiled=True).astype(F32).T
        parts = []
        for mask in (2, 3, 1, 0):
            rows = right[mask * block_rows : (mask + 1) * block_rows]
            part = lax.dot_general(left, rows, contract, preferred_element_type=F32).astype(BF16)
            parts.append(exchange(part, "tensor", mask) if mask else part)
        return sum(part.astype(F32) for part in parts)

    def sum_tensor(value):
        if not relative:
            return lax.psum(value, "tensor")
        return value + sum(exchange(value, "tensor", mask) for mask in range(1, tensor_count))

    def balance(rows, order):
        sibling = exchange(rows, "dp", 1)
        asked = order[replica_pos ^ 2]
        far = exchange(jnp.where(asked == replica_pos, rows, sibling), "dp", 2)
        source = order[replica_pos]
        return jnp.where(
            source == replica_pos, rows, jnp.where(source == replica_pos ^ 1, sibling, far)
        )

    fresh_rows = [balance(fresh[tick, 0], plan[tick]) for tick in range(TICKS)]
    fresh_documents = jnp.stack(
        [
            lax.dynamic_index_in_dim(fresh_docs[tick], plan[tick][replica_pos], 0, keepdims=False)
            for tick in range(TICKS)
        ]
    )
    gain_row = gain[0]
    gain_all = gather(gain)[0]
    out_w = assemble([gather_dp(w_out[0])])
    own_kv = jnp.stack([key_weight[0], value_weight[0]])
    for bit in range(bit_count):
        partner = exchange(own_kv, "tensor", 1 << bit)
        low_side = tensor_pos >> bit & 1 == 0
        own_kv = jnp.where(
            low_side,
            jnp.concatenate([own_kv, partner], -1),
            jnp.concatenate([partner, own_kv], -1),
        )
    query_parts = gather_dp(query_weight[0])
    forward_w = assemble([query_parts, gather_dp(own_kv[0]), gather_dp(own_kv[1])])
    if bit_count:
        grad_w = assemble([query_parts, gather_dp(key_weight[0]), gather_dp(value_weight[0])])
    else:
        grad_w = forward_w
    head_cols = own_kv.shape[2]

    def project(hidden_rows):
        hidden_f = hidden_rows.astype(F32)
        inverse = lax.rsqrt(jnp.sum(hidden_f * hidden_f, -1) / MODEL_WIDTH + NORM_EPS)
        product = jnp.dot(
            (hidden_f * gain_all).astype(BF16), forward_w, preferred_element_type=F32
        )
        return inverse, (product * inverse[:, None]).astype(BF16)

    def split(rows):
        return (
            rows[:, :query_cols],
            rows[:, query_cols : query_cols + head_cols],
            rows[:, query_cols + head_cols :],
        )

    kv_heads = head_cols // HEAD_SIZE

    def forward(hidden, documents, projected):
        parts = attention_probs(*split(projected), documents, kv_heads)
        mixed = jnp.einsum("kgij,jkd->ikgd", parts[4], parts[2], preferred_element_type=F32)
        mixed = mixed.astype(BF16).reshape(length, query_cols)
        attended = jnp.dot(gather(mixed), out_w, preferred_element_type=F32)
        return (hidden.astype(F32) + attended).astype(BF16)

    def backward(hidden, documents, grad, inverse, projected):
        query_heads, heads_of_key, heads_of_value, probs, probs_half = attention_probs(
            *split(projected), documents, kv_heads
        )
        head_gradient = product_scatter(grad, out_w).astype(BF16).reshape(query_heads.shape)
        prob_grad = jnp.einsum(
            "ikgd,jkd->kgij", head_gradient, heads_of_value, preferred_element_type=F32
        )
        score_grad = (
            probs
            * (prob_grad - jnp.sum(probs * prob_grad, axis=-1, keepdims=True))
            * HEAD_SIZE ** (-0.5)
        ).astype(BF16)
        query_grad = jnp.einsum(
            "kgij,jkd->ikgd", score_grad, heads_of_key, preferred_element_type=F32
        )
        query_grad = query_grad.astype(BF16).reshape(length, query_cols)
        key_grad = jnp.einsum(
            "kgij,ikgd->jkd", score_grad, query_heads, preferred_element_type=F32
        ).reshape(length, -1)
        value_grad = jnp.einsum(
            "kgij,ikgd->jkd", probs_half, head_gradient, preferred_element_type=F32
        ).reshape(length, -1)
        grads = jnp.concatenate([query_grad.astype(F32), key_grad, value_grad], 1)
        row_dot = sum_tensor(jnp.sum(grads * projected.astype(F32), -1)) / inverse
        kv_grad = jnp.stack([key_grad, value_grad])
        for bit in reversed(range(bit_count)):
            half = kv_grad.shape[-1] // 2
            low_side = tensor_pos >> bit & 1 == 0
            keep = jnp.where(low_side, kv_grad[..., :half], kv_grad[..., half:])
            outward = jnp.where(low_side, kv_grad[..., half:], kv_grad[..., :half])
            kv_grad = keep + exchange(outward.astype(BF16), "tensor", 1 << bit).astype(F32)
        kv_grad = kv_grad.astype(BF16)
        grad_rows = jnp.concatenate([query_grad, kv_grad[0], kv_grad[1]], axis=1)
        normed_grad = product_scatter(grad_rows, grad_w)
        hidden_f = hidden.astype(F32)
        result = (
            grad.astype(F32)
            + inverse[:, None] * (normed_grad * gain_row)
            - hidden_f * (inverse**3 * row_dot / MODEL_WIDTH)[:, None]
        )
        term = jnp.sum(normed_grad * hidden_f * inverse[:, None], axis=0)
        return result.astype(BF16), term

    outgoing = arrivals[0, 0]
    going_back = returning[0, 0]
    saved = [project(gather(stash[tick, 0, 0])) for tick in range(TICKS)]
    gain_total = jnp.zeros((width,), F32)
    for tick in range(TICKS):
        forward_in = jnp.where(section_pos == 0, fresh_rows[tick], shifted(outgoing, "section", 1))
        from_arrivals = lax.dynamic_index_in_dim(
            arrival_docs, jnp.clip(section_pos - tick - 1, 0, section_count - 1), 0, keepdims=False
        )[0]
        from_fresh = lax.dynamic_index_in_dim(
            fresh_documents, jnp.clip(tick - section_pos, 0, TICKS - 1), 0, keepdims=False
        )
        forward_docs = jnp.where(section_pos > tick, from_arrivals, from_fresh)
        grad_in = jnp.where(
            section_pos == section_count - 1,
            loss_grad[tick, 0],
            shifted(going_back, "section", -1),
        )
        outgoing = forward(forward_in, forward_docs, project(gather(forward_in))[1])
        going_back, term = backward(
            stash[tick, 0, 0], stash_docs[tick, 0, 0], grad_in, *saved[tick]
        )
        gain_total = gain_total + term
    gain_total = gain_total + exchange(gain_total, "dp", 1)
    gain_total = gain_total + exchange(gain_total, "dp", 2)
    gain_grad = gain_total / math.sqrt(TICKS * replicas * length)
    return (outgoing[None, None], going_back[None, None], gain_grad[None])


def solution(mesh):
    return jax.shard_map(
        local,
        mesh=mesh,
        in_specs=(
            P("section", "dp", None, "tensor"),
            P(None, "dp", None, "tensor"),
            P(None, "section", "dp", None, "tensor"),
            P("section", "dp", None, "tensor"),
            P(None, "dp", None, "tensor"),
            P("section", "tensor"),
            P("section", "dp", "tensor"),
            P("section", "dp", "tensor"),
            P("section", "dp", "tensor"),
            P("section", "dp", "tensor"),
            P(),
            P(),
            P(None, "dp", None),
            P(None, "section", "dp", None),
        ),
        out_specs=(
            P("section", "dp", None, "tensor"),
            P("section", "dp", None, "tensor"),
            P("section", "tensor"),
        ),
        check_vma=False,
    )
```

time: 573 us -> 423 us (0.74)
  waiting for transfers between devices: 391 us -> 153 us
  starting transfers between devices: 10.4 us -> 84.9 us
  local copies, waits for them, and re-layouts: 7.32 us -> 52.6 us
  blocking collectives: 39.8 us -> 0 us
  matrix products: 95.6 us -> 108 us
  between operations: 18.4 us -> 9.24 us
    all_gather x11 -> x0, waiting for transfers between devices: 278 us -> none  [the longest x1 59.7 us: local(): lax.all_gather(query_weight[0], 'dp', axis=0, tiled=True)]
    ppermute x4 -> x61, waiting for transfers between devices: 19.4 us -> 153 us  [the longest x57 153 us: exchange(): return lax.ppermute(block, axis, [(i, i ^ mask) for i in range(count)])]
    reduce_scatter x4 -> x0, waiting for transfers between devices: 89.8 us -> none  [the longest x2 53.5 us: local(): lax.psum_scatter(lax.dot_general(grad_weights, grad_rows, (((1,), (1,)),...]
    ppermute x4 -> x61, starting transfers between devices: 9.55 us -> 84.9 us  [the longest x57 75.5 us: exchange(): return lax.ppermute(block, axis, [(i, i ^ mask) for i in range(count)])]
    psum x4 -> x0, blocking collectives: 39.8 us -> none  [the longest x3 33.4 us: local(): lax.psum((jnp.sum(forward_f * forward_f, -1), jnp.sum(backward_f * backwa...]
    dynamic_update_slice x0 -> x16, local copies, waits for them, and re-layouts: none -> 28.4 us  [assemble(): whole = lax.dynamic_update_slice(whole, parts[mask], (row, col))]
    broadcast_in_dim x0 -> x2, local copies, waits for them, and re-layouts: none -> 9.74 us  [assemble(): whole = jnp.zeros((block_rows * replicas, cols), BF16)]
    dot_general x24 -> x36, matrix products: 95.6 us -> 105 us  [the longest x16 53.2 us: product_scatter(): lax.dot_general(left, rows, contract, preferred_element_type=F32)]
  transfers between devices with their start and end apart: 19 -> 61, of which waited for: 18 -> 22; matrix products, arithmetic and copies ran while one was open for 10% -> 39% of each run, Pallas kernels for 0% -> 0%
where the time goes in v1:
time: 423 us; the launch traced here: 420 us
  waiting for transfers between devices  153 us (36%)
  matrix products  108 us (26%)
  starting transfers between devices  84.9 us (20%)
  local copies, waits for them, and re-layouts  52.6 us (12%)
  other arithmetic  12.3 us (3%)
  between operations  9.24 us (2%)
    ppermute x57, waiting for transfers between devices, exchange(): return lax.ppermute(block, axis, [(i, i ^ mask) for i in range(count)])  153 us
    ppermute x57, starting transfers between devices, exchange(): return lax.ppermute(block, axis, [(i, i ^ mask) for i in range(count)])  75.5 us
    dot_general x16, matrix products, product_scatter(): lax.dot_general(left, rows, contract, preferred_element_type=F32)  53.2 us
    dynamic_update_slice x16, local copies, waits for them, and re-layouts, assemble(): whole = lax.dynamic_update_slice(whole, parts[mask], (row, col))  28.4 us
    dot_general x4, matrix products, project(): jnp.dot((hidden_f * gain_all).astype(BF16), forward_w, preferred_element_...  22.6 us
    dot_general x2, matrix products, forward(): attended = jnp.dot(gather(mixed), out_w, preferred_element_type=F32)  11.1 us
    broadcast_in_dim x2, local copies, waits for them, and re-layouts, assemble(): whole = jnp.zeros((block_rows * replicas, cols), BF16)  9.74 us
    ppermute x4, starting transfers between devices, shifted(): lax.ppermute(value, axis, [(source, source + steps) for source in range(l...  9.39 us
  transfers between devices with their start and end apart: 61, of which 22 were waited for; matrix products, arithmetic and copies ran while one was open for 39% of the time, Pallas kernels for 0%

profile of v1, /device:TPU:0, one launch (start us, length us, event | category | flops | bytes accessed | tf_op | source)
XLA Modules:
  0.0 419.9 jit_solution(16981898097961323873)
XLA Ops:
  0.6 5.1 %collective-permute-start.10 = (f32[1,1024]{1,0:T(1,128)}, f32[1,1024]{1,0:T(1,128)S(1)}, u32[]{:S(2)}, u32[]{:S(2)}) collective-permute-start(f32[1,1024]{1,0:T(1,128)} %param.19), channel_id=1, source_target_pairs={{0,3},{1,2},{2,1},{3,0},{4,7},{5,6},{6,5},{7,4},{8,11},{9,10},{10,... | collective-permute-start | bytes 12296 | tf_op jit(solution)/shard_map/ppermute | solution.py:20
  6.4 4.3 %collective-permute-start.4 = (bf16[128,1024]{1,0:T(8,128)(2,1)}, bf16[128,1024]{1,0:T(8,128)(2,1)}, u32[]{:S(2)}, u32[]{:S(2)}) collective-permute-start(bf16[128,1024]{1,0:T(8,128)(2,1)} %bitcast.242), channel_id=1, source_target_pairs={{0,4},{1,5},{2,6},{3,7},{8,12},{9,13},{10,14},{11,15},{16,20},{17,... | collective-permute-start | bytes 786440 | tf_op jit(solution)/shard_map/ppermute | solution.py:26
  19.1 4.3 %broadcast_in_dim.43 = bf16[4096,1024]{1,0:T(8,128)(2,1)} broadcast(bf16[]{:T(256)} %constant.69.clone.1), dimensions={} | broadcast | bytes 8388610 | tf_op jit(solution)/shard_map/broadcast_in_dim | solution.py:90
  24.9 5.4 %broadcast_in_dim.40 = bf16[4096,1536]{1,0:T(8,128)(2,1)} broadcast(bf16[]{:T(256)} %constant.69.clone.1), dimensions={} | broadcast | bytes 12582914 | tf_op jit(solution)/shard_map/broadcast_in_dim | solution.py:90
  45.5 10.4 %collective-permute-start.35 = (bf16[128,1024]{1,0:T(8,128)(2,1)S(1)}, bf16[128,1024]{1,0:T(8,128)(2,1)}, u32[]{:S(2)}, u32[]{:S(2)}) collective-permute-start(bf16[128,1024]{1,0:T(8,128)(2,1)S(1)} %get-tuple-element.7), channel_id=1, source_target_pairs={{0,2},{1,3},{2,0},{3,1},{4,6},{5,7},{6,4},{7,5},{8,10},{9,11},{10,... | collective-permute-start | bytes 786440 | tf_op jit(solution)/shard_map/ppermute | solution.py:20
  55.9 15.3 %collective-permute-done.48 = bf16[128,1024]{1,0:T(8,128)(2,1)S(1)} collective-permute-done((bf16[128,1024]{1,0:T(8,128)(2,1)S(1)}, bf16[128,1024]{1,0:T(8,128)(2,1)S(1)}, u32[]{:S(2)}, u32[]{:S(2)}) %collective-permute-start.48) | collective-permute-done | bytes 262176 | tf_op jit(solution)/shard_map/ppermute | solution.py:20
  76.3 5.9 %collective-permute-done.35 = bf16[128,1024]{1,0:T(8,128)(2,1)} collective-permute-done((bf16[128,1024]{1,0:T(8,128)(2,1)S(1)}, bf16[128,1024]{1,0:T(8,128)(2,1)}, u32[]{:S(2)}, u32[]{:S(2)}) %collective-permute-start.35) | collective-permute-done | bytes 262176 | tf_op jit(solution)/shard_map/ppermute | solution.py:20
  100.1 6.7 %collective-permute-done.7 = bf16[128,1024]{1,0:T(8,128)(2,1)S(1)} collective-permute-done((bf16[128,1024]{1,0:T(8,128)(2,1)S(1)}, bf16[128,1024]{1,0:T(8,128)(2,1)S(1)}, u32[]{:S(2)}, u32[]{:S(2)}) %collective-permute-start.7) | collective-permute-done | bytes 262176 | tf_op jit(solution)/shard_map/ppermute | solution.py:20
  106.8 4.1 collective-permute-start.6
  112.8 9.9 %collective-permute-done.6 = bf16[128,1024]{1,0:T(8,128)(2,1)S(1)} collective-permute-done((bf16[128,1024]{1,0:T(8,128)(2,1)S(1)}, bf16[128,1024]{1,0:T(8,128)(2,1)S(1)}, u32[]{:S(2)}, u32[]{:S(2)}) %collective-permute-start.6) | collective-permute-done | bytes 262176 | tf_op jit(solution)/shard_map/ppermute | solution.py:20
  124.9 5.2 %collective-permute-done.5 = bf16[128,1024]{1,0:T(8,128)(2,1)S(1)} collective-permute-done((bf16[128,1024]{1,0:T(8,128)(2,1)S(1)}, bf16[128,1024]{1,0:T(8,128)(2,1)S(1)}, u32[]{:S(2)}, u32[]{:S(2)}) %collective-permute-start.5) | collective-permute-done | bytes 262176 | tf_op jit(solution)/shard_map/ppermute | solution.py:20
  137.5 15.8 %collective-permute-done.15 = bf16[1024,256]{1,0:T(8,128)(2,1)S(1)} collective-permute-done((bf16[1024,256]{1,0:T(8,128)(2,1)S(1)}, bf16[1024,256]{1,0:T(8,128)(2,1)S(1)}, u32[]{:S(2)}, u32[]{:S(2)}) %collective-permute-start.15) | collective-permute-done | bytes 524320 | tf_op jit(solution)/shard_map/ppermute | solution.py:20
  153.4 10.0 %collective-permute-done.16 = bf16[1024,256]{1,0:T(8,128)(2,1)S(1)} collective-permute-done((bf16[1024,256]{1,0:T(8,128)(2,1)S(1)}, bf16[1024,256]{1,0:T(8,128)(2,1)S(1)}, u32[]{:S(2)}, u32[]{:S(2)}) %collective-permute-start.16) | collective-permute-done | bytes 524320 | tf_op jit(solution)/shard_map/ppermute | solution.py:20
  178.7 6.4 %fusion.18 = bf16[128,1536]{1,0:T(8,128)(2,1)S(1)} fusion(bf16[4096,1536]{1,0:T(8,128)(2,1)} %constant_dynamic-update-slice_fusion.8, f32[4096]{0:T(1024)S(1)} %bitcast.235, f32[128]{0:T(128)S(1)} %add_rsqrt_fusion.3, bf16[128,1024]{1,0:T(8,128)(2,1)S(1)} %collective-permute-done.7, bf16[128,1024]{1,0:T(8,128)(2,1)S(1)} %collective-permute-done.6, ...), kind=kOutput, calls=%fused_computation.30 | convolution fusion | flops 1616248832 | bytes 14041600 | tf_op jit(solution)/shard_map/dot_general | solution.py:162
  214.4 6.7 %fusion.21 = bf16[128,1536]{1,0:T(8,128)(2,1)S(1)} fusion(bf16[4096,1536]{1,0:T(8,128)(2,1)} %constant_dynamic-update-slice_fusion.8, f32[4096]{0:T(1024)S(1)} %bitcast.237, f32[128]{0:T(128)S(1)} %copy-done.48, bf16[128,1024]{1,0:T(8,128)(2,1)S(1)} %copy-done.18, bf16[128,1024]{1,0:T(8,128)(2,1)S(1)} %copy-done.20, bf16[128,1024]{1,0:T(8,128)(2,1)} %copy-done.21, ...), kind=kOutput, calls=%fused_computation.33 | convolution fusion | flops 1616248832 | bytes 14041600 | tf_op jit(solution)/shard_map/dot_general | solution.py:162
  227.6 10.2 %collective-permute-done.37 = bf16[128,1024]{1,0:T(8,128)(2,1)} collective-permute-done((bf16[128,1024]{1,0:T(8,128)(2,1)}, bf16[128,1024]{1,0:T(8,128)(2,1)}, u32[]{:S(2)}, u32[]{:S(2)}) %collective-permute-start.37) | collective-permute-done | bytes 262176 | tf_op jit(solution)/shard_map/ppermute | solution.py:20
  268.3 5.7 %fusion.64 = bf16[128,1024]{1,0:T(8,128)(2,1)} fusion(bf16[4096,1024]{1,0:T(8,128)(2,1)} %constant_dynamic-update-slice_fusion, bf16[128,1024]{0,1:T(8,128)(2,1)} %collective-permute-done.22, bf16[128,1024]{0,1:T(8,128)(2,1)} %collective-permute-done.21, bf16[128,1024]{0,1:T(8,128)(2,1)} %collective-permute-done.20, bf16[128,1024]{0,1:T(8,128)(2,1)} %bitcast.23, ...), kind=kOutput, calls=%fused_computation.84 | convolution fusion | flops 1078329344 | bytes 9961472 | tf_op jit(solution)/shard_map/dot_general | solution.py:180
  280.1 9.2 %collective-permute-done.40 = bf16[128,1024]{1,0:T(8,128)(2,1)S(1)} collective-permute-done((bf16[128,1024]{1,0:T(8,128)(2,1)S(1)}, bf16[128,1024]{1,0:T(8,128)(2,1)S(1)}, u32[]{:S(2)}, u32[]{:S(2)}) %collective-permute-start.40) | collective-permute-done | bytes 262176 | tf_op jit(solution)/shard_map/ppermute | solution.py:20
  311.8 8.5 %collective-permute-done.28 = bf16[128,1024]{1,0:T(8,128)(2,1)S(1)} collective-permute-done((bf16[128,1024]{1,0:T(8,128)(2,1)S(1)}, bf16[128,1024]{1,0:T(8,128)(2,1)S(1)}, u32[]{:S(2)}, u32[]{:S(2)}) %collective-permute-start.28) | collective-permute-done | bytes 262176 | tf_op jit(solution)/shard_map/ppermute | solution.py:20
  324.2 6.4 %fusion.19 = bf16[128,1536]{1,0:T(8,128)(2,1)S(1)} fusion(bf16[4096,1536]{1,0:T(8,128)(2,1)} %constant_dynamic-update-slice_fusion.8, f32[4096]{0:T(1024)S(1)} %bitcast.238, f32[128]{0:T(128)S(1)} %add_rsqrt_fusion.2, bf16[128,1024]{1,0:T(8,128)(2,1)S(1)} %collective-permute-done.29, bf16[128,1024]{1,0:T(8,128)(2,1)S(1)} %collective-permute-done.28, ...), kind=kOutput, calls=%fused_computation.31 | convolution fusion | flops 1616248832 | bytes 14041600 | tf_op jit(solution)/shard_map/dot_general | solution.py:162
  335.2 9.7 %collective-permute-done.50 = bf16[128,1024]{1,0:T(8,128)(2,1)} collective-permute-done((bf16[128,1024]{1,0:T(8,128)(2,1)S(1)}, bf16[128,1024]{1,0:T(8,128)(2,1)}, u32[]{:S(2)}, u32[]{:S(2)}) %collective-permute-start.50) | collective-permute-done | bytes 262176 | tf_op jit(solution)/shard_map/ppermute | solution.py:20
  375.7 10.3 %collective-permute-done.55 = bf16[128,1024]{1,0:T(8,128)(2,1)S(1)} collective-permute-done((bf16[128,1024]{1,0:T(8,128)(2,1)}, bf16[128,1024]{1,0:T(8,128)(2,1)S(1)}, u32[]{:S(2)}, u32[]{:S(2)}) %collective-permute-start.55) | collective-permute-done | bytes 262176 | tf_op jit(solution)/shard_map/ppermute | solution.py:20
  386.1 20.0 %collective-permute-done.53 = bf16[128,1024]{1,0:T(8,128)(2,1)} collective-permute-done((bf16[128,1024]{1,0:T(8,128)(2,1)}, bf16[128,1024]{1,0:T(8,128)(2,1)}, u32[]{:S(2)}, u32[]{:S(2)}) %collective-permute-start.53) | collective-permute-done | bytes 262176 | tf_op jit(solution)/shard_map/ppermute | solution.py:20
  413.9 5.4 %fusion.146 = bf16[1,1,128,1024]{3,2,1,0:T(8,128)(2,1)} fusion(bf16[4096,1024]{1,0:T(8,128)(2,1)} %constant_dynamic-update-slice_fusion, bf16[128,1024]{0,1:T(8,128)(2,1)S(1)} %collective-permute-done.32, bf16[128,1024]{0,1:T(8,128)(2,1)S(1)} %collective-permute-done.31, bf16[128,1024]{0,1:T(8,128)(2,1)S(1)} %collective-permute-done.30, ...), kind=kOutput, calls=%fused_computation.118 | convolution fusion | flops 1078329344 | bytes 9961472 | tf_op jit(solution)/shard_map/dot_general | solution.py:180
  (332 shorter events, 209.7 us)
Async XLA Ops:
  0.6 32.5 %collective-permute-start.10 = (f32[1,1024]{1,0:T(1,128)}, f32[1,1024]{1,0:T(1,128)S(1)}, u32[]{:S(2)}, u32[]{:S(2)}) collective-permute-start(f32[1,1024]{1,0:T(1,128)} %param.19), channel_id=1, source_target_pairs={{0,3},{1,2},{2,1},{3,0},{4,7},{5,6},{6,5},{7,4},{8,11},{9,10},{10,... | collective-permute-start | bytes 12296 | tf_op jit(solution)/shard_map/ppermute | solution.py:20
  5.8 31.3 %collective-permute-start.9 = (f32[1,1024]{1,0:T(1,128)}, f32[1,1024]{1,0:T(1,128)S(1)}, u32[]{:S(2)}, u32[]{:S(2)}) collective-permute-start(f32[1,1024]{1,0:T(1,128)} %param.19), channel_id=1, source_target_pairs={{0,2},{1,3},{2,0},{3,1},{4,6},{5,7},{6,4},{7,5},{8,10},{9,11},{10,... | collective-permute-start | bytes 12296 | tf_op jit(solution)/shard_map/ppermute | solution.py:20
  5.8 31.3 %collective-permute-start.8 = (f32[1,1024]{1,0:T(1,128)}, f32[1,1024]{1,0:T(1,128)S(1)}, u32[]{:S(2)}, u32[]{:S(2)}) collective-permute-start(f32[1,1024]{1,0:T(1,128)} %param.19), channel_id=1, source_target_pairs={{0,1},{1,0},{2,3},{3,2},{4,5},{5,4},{6,7},{7,6},{8,9},{9,8},{10,11... | collective-permute-start | bytes 12296 | tf_op jit(solution)/shard_map/ppermute | solution.py:20
  6.4 31.3 %collective-permute-start.4 = (bf16[128,1024]{1,0:T(8,128)(2,1)}, bf16[128,1024]{1,0:T(8,128)(2,1)}, u32[]{:S(2)}, u32[]{:S(2)}) collective-permute-start(bf16[128,1024]{1,0:T(8,128)(2,1)} %bitcast.242), channel_id=1, source_target_pairs={{0,4},{1,5},{2,6},{3,7},{8,12},{9,13},{10,14},{11,15},{16,20},{17,... | collective-permute-start | bytes 786440 | tf_op jit(solution)/shard_map/ppermute | solution.py:26
  12.5 26.8 %collective-permute-start.2 = (bf16[128,1024]{1,0:T(8,128)(2,1)}, bf16[128,1024]{1,0:T(8,128)(2,1)S(1)}, u32[]{:S(2)}, u32[]{:S(2)}) collective-permute-start(bf16[128,1024]{1,0:T(8,128)(2,1)} %get-tuple-element.11), channel_id=1, source_target_pairs={{0,8},{8,0},{16,24},{24,16},{1,9},{9,1},{17,25},{25,17},{2,10},{10... | collective-permute-start | bytes 786440 | tf_op jit(solution)/shard_map/ppermute | solution.py:20
  37.0 34.2 %collective-permute-start.48 = (bf16[128,1024]{1,0:T(8,128)(2,1)S(1)}, bf16[128,1024]{1,0:T(8,128)(2,1)S(1)}, u32[]{:S(2)}, u32[]{:S(2)}) collective-permute-start(bf16[128,1024]{1,0:T(8,128)(2,1)S(1)} %get-tuple-element.6), channel_id=1, source_target_pairs={{0,2},{1,3},{2,0},{3,1},{4,6},{5,7},{6,4},{7,5},{8,10},{9,11},{10,... | collective-permute-start | bytes 786440 | tf_op jit(solution)/shard_map/ppermute | solution.py:20
  37.0 34.2 %collective-permute-start.47 = (bf16[128,1024]{1,0:T(8,128)(2,1)S(1)}, bf16[128,1024]{1,0:T(8,128)(2,1)S(1)}, u32[]{:S(2)}, u32[]{:S(2)}) collective-permute-start(bf16[128,1024]{1,0:T(8,128)(2,1)S(1)} %get-tuple-element.6), channel_id=1, source_target_pairs={{0,1},{1,0},{2,3},{3,2},{4,5},{5,4},{6,7},{7,6},{8,9},{9,8},{10,11... | collective-permute-start | bytes 786440 | tf_op jit(solution)/shard_map/ppermute | solution.py:20
  37.7 73.2 %collective-permute-start.14 = (bf16[1024,1024]{1,0:T(8,128)(2,1)S(1)}, bf16[1024,1024]{1,0:T(8,128)(2,1)}, u32[]{:S(2)}, u32[]{:S(2)}) collective-permute-start(bf16[1024,1024]{1,0:T(8,128)(2,1)S(1)} %bitcast.199), channel_id=1, source_target_pairs={{0,16},{8,24},{16,0},{24,8},{1,17},{9,25},{17,1},{25,9},{2,18},{10... | collective-permute-start | bytes 6291464 | tf_op jit(solution)/shard_map/ppermute | solution.py:20
  42.0 34.2 %collective-permute-start.36 = (bf16[128,1024]{1,0:T(8,128)(2,1)S(1)}, bf16[128,1024]{1,0:T(8,128)(2,1)}, u32[]{:S(2)}, u32[]{:S(2)}) collective-permute-start(bf16[128,1024]{1,0:T(8,128)(2,1)S(1)} %get-tuple-element.7), channel_id=1, source_target_pairs={{0,3},{1,2},{2,1},{3,0},{4,7},{5,6},{6,5},{7,4},{8,11},{9,10},{10,... | collective-permute-start | bytes 786440 | tf_op jit(solution)/shard_map/ppermute | solution.py:20
  45.5 36.7 %collective-permute-start.35 = (bf16[128,1024]{1,0:T(8,128)(2,1)S(1)}, bf16[128,1024]{1,0:T(8,128)(2,1)}, u32[]{:S(2)}, u32[]{:S(2)}) collective-permute-start(bf16[128,1024]{1,0:T(8,128)(2,1)S(1)} %get-tuple-element.7), channel_id=1, source_target_pairs={{0,2},{1,3},{2,0},{3,1},{4,6},{5,7},{6,4},{7,5},{8,10},{9,11},{10,... | collective-permute-start | bytes 786440 | tf_op jit(solution)/shard_map/ppermute | solution.py:20
  76.1 54.6 %collective-permute-start.11 = (bf16[1024,1024]{1,0:T(8,128)(2,1)S(1)}, bf16[1024,1024]{1,0:T(8,128)(2,1)}, u32[]{:S(2)}, u32[]{:S(2)}) collective-permute-start(bf16[1024,1024]{1,0:T(8,128)(2,1)S(1)} %bitcast.200), channel_id=1, source_target_pairs={{0,8},{8,0},{16,24},{24,16},{1,9},{9,1},{17,25},{25,17},{2,10},{10... | collective-permute-start | bytes 6291464 | tf_op jit(solution)/shard_map/ppermute | solution.py:20
  93.4 69.9 %collective-permute-start.24 = (bf16[1024,1024]{1,0:T(8,128)(2,1)}, bf16[1024,1024]{1,0:T(8,128)(2,1)}, u32[]{:S(2)}, u32[]{:S(2)}) collective-permute-start(bf16[1024,1024]{1,0:T(8,128)(2,1)} %bitcast.201), channel_id=1, source_target_pairs={{0,16},{8,24},{16,0},{24,8},{1,17},{9,25},{17,1},{25,9},{2,18},{10... | collective-permute-start | bytes 6291464 | tf_op jit(solution)/shard_map/ppermute | solution.py:20
  96.1 69.7 %collective-permute-start.23 = (bf16[1024,1024]{1,0:T(8,128)(2,1)S(1)}, bf16[1024,1024]{1,0:T(8,128)(2,1)S(1)}, u32[]{:S(2)}, u32[]{:S(2)}) collective-permute-start(bf16[1024,1024]{1,0:T(8,128)(2,1)S(1)} %bitcast.202), channel_id=1, source_target_pairs={{0,8},{8,0},{16,24},{24,16},{1,9},{9,1},{17,25},{25,17},{2,10},{10... | collective-permute-start | bytes 6291464 | tf_op jit(solution)/shard_map/ppermute | solution.py:20
  110.9 64.4 %collective-permute-start.17 = (bf16[1024,1024]{1,0:T(8,128)(2,1)}, bf16[1024,1024]{1,0:T(8,128)(2,1)S(1)}, u32[]{:S(2)}, u32[]{:S(2)}) collective-permute-start(bf16[1024,1024]{1,0:T(8,128)(2,1)} %collective-permute-done.14), channel_id=1, source_target_pairs={{0,8},{8,0},{16,24},{24,16},{1,9},{9,1},{17,25},{25,17},{2,10},{10... | collective-permute-start | bytes 6291464 | tf_op jit(solution)/shard_map/ppermute | solution.py:20
  130.7 32.6 %collective-permute-start.16 = (bf16[1024,256]{1,0:T(8,128)(2,1)S(1)}, bf16[1024,256]{1,0:T(8,128)(2,1)S(1)}, u32[]{:S(2)}, u32[]{:S(2)}) collective-permute-start(bf16[1024,256]{1,0:T(8,128)(2,1)S(1)} %bitcast.216), channel_id=1, source_target_pairs={{0,16},{8,24},{16,0},{24,8},{1,17},{9,25},{17,1},{25,9},{2,18},{10... | collective-permute-start | bytes 1572872 | tf_op jit(solution)/shard_map/ppermute | solution.py:20
  163.3 30.0 %collective-permute-start.25 = (bf16[1024,1024]{1,0:T(8,128)(2,1)}, bf16[1024,1024]{1,0:T(8,128)(2,1)S(1)}, u32[]{:S(2)}, u32[]{:S(2)}) collective-permute-start(bf16[1024,1024]{1,0:T(8,128)(2,1)} %collective-permute-done.24), channel_id=1, source_target_pairs={{0,8},{8,0},{16,24},{24,16},{1,9},{9,1},{17,25},{25,17},{2,10},{10... | collective-permute-start | bytes 6291464 | tf_op jit(solution)/shard_map/ppermute | solution.py:20
  191.0 71.7 %collective-permute-start.22 = (bf16[128,1024]{0,1:T(8,128)(2,1)}, bf16[128,1024]{0,1:T(8,128)(2,1)}, u32[]{:S(2)}, u32[]{:S(2)}) collective-permute-start(bf16[128,1024]{0,1:T(8,128)(2,1)} %bitcast.23), channel_id=1, source_target_pairs={{0,3},{1,2},{2,1},{3,0},{4,7},{5,6},{6,5},{7,4},{8,11},{9,10},{10,... | collective-permute-start | bytes 786440 | tf_op jit(solution)/shard_map/ppermute | solution.py:20
  193.3 71.5 %collective-permute-start.21 = (bf16[128,1024]{0,1:T(8,128)(2,1)}, bf16[128,1024]{0,1:T(8,128)(2,1)}, u32[]{:S(2)}, u32[]{:S(2)}) collective-permute-start(bf16[128,1024]{0,1:T(8,128)(2,1)} %bitcast.23), channel_id=1, source_target_pairs={{0,2},{1,3},{2,0},{3,1},{4,6},{5,7},{6,4},{7,5},{8,10},{9,11},{10,... | collective-permute-start | bytes 786440 | tf_op jit(solution)/shard_map/ppermute | solution.py:20
  226.0 38.9 %collective-permute-start.20 = (bf16[128,1024]{0,1:T(8,128)(2,1)}, bf16[128,1024]{0,1:T(8,128)(2,1)}, u32[]{:S(2)}, u32[]{:S(2)}) collective-permute-start(bf16[128,1024]{0,1:T(8,128)(2,1)} %bitcast.23), channel_id=1, source_target_pairs={{0,1},{1,0},{2,3},{3,2},{4,5},{5,4},{6,7},{7,6},{8,9},{9,8},{10,11... | collective-permute-start | bytes 786440 | tf_op jit(solution)/shard_map/ppermute | solution.py:20
  274.0 23.6 %collective-permute-start.1 = (bf16[128,1024]{1,0:T(8,128)(2,1)S(1)}, bf16[128,1024]{1,0:T(8,128)(2,1)}, u32[]{:S(2)}, u32[]{:S(2)}) collective-permute-start(bf16[128,1024]{1,0:T(8,128)(2,1)S(1)} %copy-done.16), channel_id=1, source_target_pairs={{0,16},{8,24},{16,0},{24,8},{1,17},{9,25},{17,1},{25,9},{2,18},{10... | collective-permute-start | bytes 786440 | tf_op jit(solution)/shard_map/ppermute | solution.py:20
  370.5 35.6 %collective-permute-start.53 = (bf16[128,1024]{1,0:T(8,128)(2,1)}, bf16[128,1024]{1,0:T(8,128)(2,1)}, u32[]{:S(2)}, u32[]{:S(2)}) collective-permute-start(bf16[128,1024]{1,0:T(8,128)(2,1)} %fusion.107), channel_id=1, source_target_pairs={{0,2},{1,3},{2,0},{3,1},{4,6},{5,7},{6,4},{7,5},{8,10},{9,11},{10,... | collective-permute-start | bytes 786440 | tf_op jit(solution)/shard_map/ppermute | solution.py:20
  373.3 40.4 %collective-permute-start.32 = (bf16[128,1024]{0,1:T(8,128)(2,1)S(1)}, bf16[128,1024]{0,1:T(8,128)(2,1)S(1)}, u32[]{:S(2)}, u32[]{:S(2)}) collective-permute-start(bf16[128,1024]{0,1:T(8,128)(2,1)S(1)} %bitcast.244), channel_id=1, source_target_pairs={{0,3},{1,2},{2,1},{3,0},{4,7},{5,6},{6,5},{7,4},{8,11},{9,10},{10,... | collective-permute-start | bytes 786440 | tf_op jit(solution)/shard_map/ppermute | solution.py:20
  375.5 38.4 %collective-permute-start.31 = (bf16[128,1024]{0,1:T(8,128)(2,1)S(1)}, bf16[128,1024]{0,1:T(8,128)(2,1)S(1)}, u32[]{:S(2)}, u32[]{:S(2)}) collective-permute-start(bf16[128,1024]{0,1:T(8,128)(2,1)S(1)} %bitcast.245), channel_id=1, source_target_pairs={{0,2},{1,3},{2,0},{3,1},{4,6},{5,7},{6,4},{7,5},{8,10},{9,11},{10,... | collective-permute-start | bytes 786440 | tf_op jit(solution)/shard_map/ppermute | solution.py:20
  386.0 27.9 %collective-permute-start.30 = (bf16[128,1024]{0,1:T(8,128)(2,1)S(1)}, bf16[128,1024]{0,1:T(8,128)(2,1)S(1)}, u32[]{:S(2)}, u32[]{:S(2)}) collective-permute-start(bf16[128,1024]{0,1:T(8,128)(2,1)S(1)} %bitcast.246), channel_id=1, source_target_pairs={{0,1},{1,0},{2,3},{3,2},{4,5},{5,4},{6,7},{7,6},{8,9},{9,8},{10,11... | collective-permute-start | bytes 786440 | tf_op jit(solution)/shard_map/ppermute | solution.py:20
  (90 other events, 1595.0 us)

commit v2 on v1

v2 whole, which is shorter than its diff:
```python
import functools
import math

import jax
import jax.numpy as jnp
from jax import lax
from jax.experimental import pallas as pl
from jax.experimental.pallas import tpu as pltpu
from jax.sharding import PartitionSpec as P

MODEL_WIDTH = 4096
QUERY_HEADS = 32
KEY_VALUE_HEADS = 8
HEAD_SIZE = 128
TICKS = 2
NORM_EPS = 1e-05
F32 = jnp.float32
BF16 = jnp.bfloat16


NEAR = (((1,), (1,)), ((), ()))
FIRST = (((0,), (0,)), ((), ()))
CHUNKS = 2
VMEM = 32 * 2**20


def exchange(block, axis, mask):
    count = lax.axis_size(axis)
    return lax.ppermute(block, axis, [(i, i ^ mask) for i in range(count)])


def shifted(value, axis, steps):
    count = lax.axis_size(axis)
    leading, last = (max(0, -steps), min(count, count - steps))
    return lax.ppermute(value, axis, [(source, source + steps) for source in range(leading, last)])


def dot(left, right, contract=(((1,), (0,)), ((), ()))):
    return lax.dot_general(left, right, contract, preferred_element_type=F32)


def call(kernel, args, outs, scratch=(), specs=None, after=()):

    def whole(dims):
        return pl.BlockSpec(dims, lambda step: (0,) * len(dims))

    def body(*refs):
        kernel(*refs[: len(args)], *refs[len(args) + len(after) :])

    return pl.pallas_call(
        body,
        grid=(1,),
        in_specs=[
            spec if spec is not None else whole(a.shape)
            for spec, a in zip(specs or [None] * len(args), args)
        ]
        + [pl.BlockSpec(memory_space=pl.ANY)] * len(after),
        out_specs=[whole(o.shape) for o in outs],
        out_shape=[jax.ShapeDtypeStruct(o.shape, o.dtype) for o in outs],
        scratch_shapes=list(scratch),
        compiler_params=pltpu.CompilerParams(vmem_limit_bytes=VMEM),
        cost_estimate=pl.CostEstimate(flops=1024, bytes_accessed=1024, transcendentals=0),
    )(*args, *after)


def tie(value, *after):
    def body(*refs):
        pass

    return pl.pallas_call(
        body,
        in_specs=[pl.BlockSpec(memory_space=pl.ANY)] * (1 + len(after)),
        out_specs=pl.BlockSpec(memory_space=pl.ANY),
        out_shape=jax.ShapeDtypeStruct(value.shape, value.dtype),
        input_output_aliases={0: 0},
        cost_estimate=pl.CostEstimate(flops=0, bytes_accessed=0, transcendentals=0),
    )(value, *after)


def shape(rows, cols, dtype=F32):
    return jax.ShapeDtypeStruct((rows, cols), dtype)


class Loader:
    def __init__(self, which_ref, groups, buffers, sems, count):
        self.groups, self.buffers, self.sems = groups, buffers, sems
        for i in range(count):
            for chunk in range(CHUNKS):
                for group, parts in enumerate(groups):
                    for k, part in enumerate(parts):
                        pl.when(which_ref[i] == k)(self.copy(part, group, i, chunk).start)

    def copy(self, part, group, i, chunk):
        rows = part.shape[0] // CHUNKS
        at = pl.ds(chunk * rows, rows)
        return pltpu.make_async_copy(
            part.at[at], self.buffers[group].at[i, at], self.sems.at[group, i, chunk]
        )

    def wait(self, group, i, chunk):
        self.copy(self.groups[group][0], group, i, chunk).wait()


def load_scratch(groups, count):
    return [pltpu.VMEM((count,) + parts[0].shape, BF16) for parts in groups] + [
        pltpu.SemaphoreType.DMA((len(groups), count, CHUNKS))
    ]


def sum_kernel(count, sizes, has_gains, has_before, final, *refs):
    refs = list(refs)
    take = lambda n: [refs.pop(0) for _ in range(n)]
    (which,) = take(1)
    blocks = take(count)
    gains = take(count) if has_gains else []
    groups = [take(size) for size in sizes]
    totals_in = take(len(sizes) + has_gains) if has_before else []
    hidden = take(1) if final else []
    totals = take(len(sizes) + has_gains)
    loader = Loader(which, groups, take(len(sizes)), refs.pop(), count)
    squares = totals_in[-1][...] if has_gains and has_before else 0.0
    running = {}
    for i in range(count):
        block = blocks[i][...]
        if has_gains:
            block = block.astype(F32)
            squares = squares + jnp.sum(block * block, axis=-1, keepdims=True)
            block = (block * gains[i][...]).astype(BF16)
        rows = block.shape[1] // CHUNKS
        for chunk in range(CHUNKS):
            for group in range(len(sizes)):
                loader.wait(group, i, chunk)
                at = slice(chunk * rows, (chunk + 1) * rows)
                term = dot(block[:, at], loader.buffers[group][i, at])
                if i or chunk:
                    term = term + running[group]
                elif has_before:
                    term = term + totals_in[group][...]
                running[group] = term
    for group in range(len(sizes)):
        if final:
            totals[group][...] = (running[group] + hidden[0][...].astype(F32)).astype(BF16)
        else:
            totals[group][...] = running[group]
    if has_gains:
        totals[-1][...] = squares


def sum_of(which, blocks, groups, gains=(), before=(), hidden=None, after=()):
    length = blocks[0].shape[0]
    args = [which, *blocks, *gains]
    specs = [pl.BlockSpec(memory_space=pltpu.SMEM)] + [None] * (len(args) - 1)
    for parts in groups:
        args += parts
        specs += [pl.BlockSpec(memory_space=pl.ANY)] * len(parts)
    args += [*before] + ([] if hidden is None else [hidden])
    specs += [None] * (len(args) - len(specs))
    outs = [
        shape(length, parts[0].shape[1], F32 if hidden is None else BF16) for parts in groups
    ] + ([shape(length, 1)] if gains else [])
    return call(
        functools.partial(
            sum_kernel,
            len(blocks),
            [len(parts) for parts in groups],
            bool(gains),
            bool(before),
            hidden is not None,
        ),
        args,
        outs,
        load_scratch(groups, len(blocks)),
        specs,
        after,
    )


def turned_kernel(sizes, count, has_aside, *refs):
    refs = list(refs)
    take = lambda n: [refs.pop(0) for _ in range(n)]
    (which,) = take(1)
    lefts = take(len(sizes))
    groups = [take(size) for size in sizes]
    aside = take(1) if has_aside else []
    outs = take(count)
    loader = Loader(which, groups, take(len(sizes)), refs.pop(), count)
    width = groups[0][0].shape[0]
    rows = width // CHUNKS
    for i, out in enumerate(outs):
        for chunk in range(CHUNKS):
            at = slice(chunk * rows, (chunk + 1) * rows)
            total = 0.0
            for group, left in enumerate(lefts):
                loader.wait(group, i, chunk)
                total = total + dot(left[...], loader.buffers[group][i, at], NEAR)
            out[:, at] = total.astype(out.dtype)
    if has_aside:
        outs[0][:, width:] = aside[0][...]


def turned_products(which, lefts, groups, dtypes, aside=None, after=()):
    args = [which, *lefts]
    specs = [pl.BlockSpec(memory_space=pltpu.SMEM)] + [None] * len(lefts)
    for parts in groups:
        args += parts
        specs += [pl.BlockSpec(memory_space=pl.ANY)] * len(parts)
    args += [] if aside is None else [aside]
    specs += [None] * (len(args) - len(specs))
    width = groups[0][0].shape[0]
    outs = [shape(lefts[0].shape[0], width, dtype) for dtype in dtypes]
    if aside is not None:
        outs[0] = shape(lefts[0].shape[0], width + aside.shape[1], dtypes[0])
    return call(
        functools.partial(
            turned_kernel, [len(parts) for parts in groups], len(dtypes), aside is not None
        ),
        args,
        outs,
        load_scratch(groups, len(dtypes)),
        specs,
        after,
    )


def joined_kernel(part_ref, last_ref, *refs):
    out = refs[-1]
    width = part_ref.shape[1]
    out[:, :width] = (part_ref[...] + last_ref[:, :width].astype(F32)).astype(BF16)
    if len(refs) > 1:
        value = refs[0][...].astype(F32) + last_ref[:, width:].astype(F32)
        out[:, width:] = two_lanes(value[:, :1] + value[:, 1:2], value.shape)


def two_lanes(value, dims):
    high = value.astype(BF16).astype(F32)
    lane = lax.broadcasted_iota(jnp.int32, dims, 1)
    return jnp.where(lane == 0, high, jnp.where(lane == 1, value - high, 0.0)).astype(BF16)


def stacked(value, first, per_key):
    return jnp.concatenate(
        [value[:, (first + a) * HEAD_SIZE : (first + a + 1) * HEAD_SIZE] for a in range(per_key)], 0
    )


def masked_probs(rows, keys, docs_down, docs_across, per_key):
    length = keys.shape[0]
    scores = dot(rows, keys, NEAR) * HEAD_SIZE ** (-0.5)
    down = lax.broadcasted_iota(jnp.int32, (length, length), 0)
    across = lax.broadcasted_iota(jnp.int32, (length, length), 1)
    allowed = jnp.logical_and(docs_down[...] == docs_across[...], down >= across)
    allowed = jnp.concatenate([allowed.astype(F32)] * per_key, 0) > 0.5
    raised = jnp.where(allowed, jnp.exp(scores), 0.0)
    return raised / jnp.sum(raised, axis=-1, keepdims=True)


def normed_rows(query_ref, kv_ref, squares_ref):
    inverse = lax.rsqrt(squares_ref[...] / MODEL_WIDTH + NORM_EPS)
    return (query_ref[...] * inverse).astype(BF16), (kv_ref[...] * inverse).astype(BF16)


def forward_heads(kv_heads, query_ref, kv_ref, squares_ref, down_ref, across_ref, mixed_ref):
    length, query_cols = mixed_ref.shape
    per_key = query_cols // (kv_heads * HEAD_SIZE)
    queries, kv = normed_rows(query_ref, kv_ref, squares_ref)
    for head in range(kv_heads):
        key_at = head * HEAD_SIZE
        value_at = key_at + kv_heads * HEAD_SIZE
        query = stacked(queries, head * per_key, per_key)
        keys = kv[:, key_at : key_at + HEAD_SIZE]
        probs = masked_probs(query, keys, down_ref, across_ref, per_key)
        mixed = dot(probs.astype(BF16), kv[:, value_at : value_at + HEAD_SIZE]).astype(BF16)
        for a in range(per_key):
            at = (head * per_key + a) * HEAD_SIZE
            mixed_ref[:, at : at + HEAD_SIZE] = mixed[a * length : (a + 1) * length]


def backward_heads(kv_heads, count, rows_ref, kv_rows_ref, squares_ref, down_ref, across_ref, *refs):
    terms, (query_ref, kv_ref, dot_ref) = refs[:count], refs[count:]
    length, query_cols = query_ref.shape
    per_key = query_cols // (kv_heads * HEAD_SIZE)
    queries, kv = normed_rows(rows_ref, kv_rows_ref, squares_ref)
    total = terms[0][...].astype(F32)
    for term in terms[1:]:
        total = total + term[...].astype(F32)
    grads = total.astype(BF16)
    row_dot = jnp.zeros((length, 1), F32)
    for head in range(kv_heads):
        key_at = head * HEAD_SIZE
        value_at = key_at + kv_heads * HEAD_SIZE
        query = stacked(queries, head * per_key, per_key)
        keys = kv[:, key_at : key_at + HEAD_SIZE]
        values = kv[:, value_at : value_at + HEAD_SIZE]
        probs = masked_probs(query, keys, down_ref, across_ref, per_key)
        grad = stacked(grads, head * per_key, per_key)
        prob_grad = dot(grad, values, NEAR)
        inner = jnp.sum(probs * prob_grad, axis=-1, keepdims=True)
        score_grad = (probs * (prob_grad - inner) * HEAD_SIZE ** (-0.5)).astype(BF16)
        query_grad = dot(score_grad, keys)
        key_grad = dot(score_grad, query, FIRST)
        value_grad = dot(probs.astype(BF16), grad, FIRST)
        products = jnp.sum(query_grad * query.astype(F32), axis=-1, keepdims=True)
        for a in range(per_key):
            at = (head * per_key + a) * HEAD_SIZE
            rows = slice(a * length, (a + 1) * length)
            query_ref[:, at : at + HEAD_SIZE] = query_grad[rows].astype(BF16)
            row_dot = row_dot + products[rows]
        row_dot = row_dot + jnp.sum(key_grad * keys.astype(F32), axis=-1, keepdims=True)
        row_dot = row_dot + jnp.sum(value_grad * values.astype(F32), axis=-1, keepdims=True)
        kv_ref[:, key_at : key_at + HEAD_SIZE] = key_grad.astype(kv_ref.dtype)
        kv_ref[:, value_at : value_at + HEAD_SIZE] = value_grad.astype(kv_ref.dtype)
    dot_ref[...] = two_lanes(row_dot, dot_ref.shape)


def split_float(value):
    high = lax.reduce_precision(value, 8, 7)
    middle = lax.reduce_precision(value - high, 8, 7)
    return [high.astype(BF16), middle.astype(BF16), (value - high - middle).astype(BF16)]


def local(
    arrivals,
    fresh,
    stash,
    returning,
    loss_grad,
    gain,
    query_weight,
    key_weight,
    value_weight,
    w_out,
    plan,
    fresh_docs,
    arrival_docs,
    stash_docs,
):
    tensor_count = lax.axis_size("tensor")
    section_count = lax.axis_size("section")
    replicas = lax.axis_size("dp")
    tensor_pos = lax.axis_index("tensor")
    section_pos = lax.axis_index("section")
    replica_pos = lax.axis_index("dp")
    length, width = arrivals.shape[2:]
    heads_here = QUERY_HEADS // tensor_count
    group_width = QUERY_HEADS // KEY_VALUE_HEADS
    share_count = max(1, group_width // heads_here)
    bit_count = share_count.bit_length() - 1
    query_cols = heads_here * HEAD_SIZE
    block_rows = query_weight.shape[1]
    relative = tensor_count == replicas
    shift = tensor_pos if relative else 0
    which = [(replica_pos ^ mask ^ shift).astype(jnp.int32) for mask in range(replicas)]

    def picks(*masks):
        return jnp.stack([which[mask] for mask in masks])

    def fixed(*masks):
        return jnp.array(masks, jnp.int32)

    def gather_dp(weight):
        other = exchange(weight, "dp", 2)
        sibling = exchange(weight, "dp", 1)
        return [weight, sibling, other, exchange(other, "dp", 1)]

    def gather(block):
        if not relative:
            whole = lax.all_gather(block, "tensor", axis=1, tiled=True)
            return jnp.split(whole, replicas, 1)
        far = exchange(block, "tensor", 2)
        near = exchange(block, "tensor", 1)
        return [block, near, far, exchange(far, "tensor", 1)]

    def product_scatter(lefts, groups, aside=None, after=()):
        if not relative:
            part = turned_products(picks(0, 1, 2, 3), lefts, groups, [BF16] * 4)
            part = jnp.concatenate(part, 1)
            terms = [lax.psum_scatter(part, "tensor", scatter_dimension=1, tiled=True)]
            if aside is None:
                return terms
            return terms, lax.psum(aside[:, :1].astype(F32) + aside[:, 1:2].astype(F32), "tensor")
        (last,) = turned_products(picks(3), lefts, groups, [BF16], aside, after)
        near, far = turned_products(picks(1, 2), lefts, groups, [BF16, F32], None, [last])
        last = exchange(last, "tensor", 1)
        near = exchange(near, "tensor", 1)
        asides = [] if aside is None else [aside]
        (joined,) = call(
            joined_kernel, [far, last, *asides], [shape(length, last.shape[1], BF16)]
        )
        far = exchange(joined, "tensor", 2)
        (own,) = turned_products(picks(0), lefts, groups, [BF16], None, [joined])
        terms = [own, near, far[:, :block_rows]]
        if aside is None:
            return terms
        sides = [aside, last[:, block_rows:], far[:, block_rows:]]
        return terms, sum(
            side[:, i : i + 1].astype(F32) for side in sides for i in range(2)
        )

    def balance(rows):
        sibling = exchange(rows, "dp", 1)
        asked = plan[:, replica_pos ^ 2][:, None, None]
        source = plan[:, replica_pos][:, None, None]
        far = exchange(jnp.where(asked == replica_pos, rows, sibling), "dp", 2)
        return jnp.where(
            source == replica_pos, rows, jnp.where(source == replica_pos ^ 1, sibling, far)
        )

    balanced = balance(fresh[:, 0])
    own_kv = [key_weight[0], value_weight[0]]
    pair_kv = own_kv
    for bit in range(bit_count):
        low_side = tensor_pos >> bit & 1 == 0
        partners = [exchange(block, "tensor", 1 << bit) for block in pair_kv]
        pair_kv = [
            jnp.where(
                low_side,
                jnp.concatenate([block, partner], -1),
                jnp.concatenate([partner, block], -1),
            )
            for block, partner in zip(pair_kv, partners)
        ]
    head_cols = pair_kv[0].shape[1]
    kv_heads = head_cols // HEAD_SIZE
    kv_weight = jnp.concatenate(pair_kv, 1)
    out_x, kv_x, query_x = [
        exchange(weight, "dp", 2) for weight in (w_out[0], kv_weight, query_weight[0])
    ]
    out_sibling, kv_sibling, query_sibling = [
        exchange(weight, "dp", 1) for weight in (w_out[0], kv_weight, query_weight[0])
    ]

    def far_dp(weight, sibling, other):
        return [weight, sibling, other, exchange(other, "dp", 1)]

    gain_row = gain[0]

    def attend(kernel, outs, sums, group, documents, terms=(), after=()):
        row = [pl.BlockSpec((length, a.shape[1]), lambda step: (group, 0)) for a in sums]
        args = (*sums, documents[:, None], documents[None, :], *terms)
        return call(kernel, args, outs, (), row + [None] * (2 + len(terms)), after)

    def mix(documents, sums, group):
        (mixed,) = attend(
            functools.partial(forward_heads, kv_heads),
            [shape(length, query_cols, BF16)],
            sums,
            group,
            documents,
        )
        return mixed

    def project_out(hidden, blocks, after=()):
        before = sum_of(picks(0, 1, 2), blocks[:3], [out_parts], after=after)
        return sum_of(picks(3), blocks[3:], [out_parts], (), before, hidden)[0]

    def head_terms(grad, after=()):
        return product_scatter([grad], [out_parts], None, after)

    def backward(hidden, documents, grad, terms, sums, group, after=()):
        query_grad, kv_grad, aside = attend(
            functools.partial(backward_heads, kv_heads, len(terms)),
            [
                shape(length, query_cols, BF16),
                shape(length, 2 * head_cols, F32 if bit_count else BF16),
                shape(length, HEAD_SIZE, BF16),
            ],
            sums,
            group,
            documents,
            terms,
            after,
        )
        if bit_count:
            kv_grad = jnp.stack([kv_grad[:, :head_cols], kv_grad[:, head_cols:]])
            for bit in reversed(range(bit_count)):
                half = kv_grad.shape[-1] // 2
                low_side = tensor_pos >> bit & 1 == 0
                keep = jnp.where(low_side, kv_grad[..., :half], kv_grad[..., half:])
                outward = jnp.where(low_side, kv_grad[..., half:], kv_grad[..., :half])
                kv_grad = keep + exchange(outward.astype(BF16), "tensor", 1 << bit).astype(F32)
            kv_grad = jnp.concatenate([kv_grad[0], kv_grad[1]], 1).astype(BF16)
        terms, row_dot = product_scatter(
            [query_grad, kv_grad], [query_parts, grad_kv_parts], aside
        )
        normed_grad = sum(term.astype(F32) for term in terms)
        squares = sums[2][group * length : (group + 1) * length]
        inverse = lax.rsqrt(squares / MODEL_WIDTH + NORM_EPS)
        row_dot = row_dot / inverse
        hidden_f = hidden.astype(F32)
        result = (
            grad.astype(F32)
            + inverse * (normed_grad * gain_row)
            - hidden_f * (inverse**3 * row_dot / MODEL_WIDTH)
        )
        term = jnp.sum(normed_grad * hidden_f * inverse, axis=0)
        return result.astype(BF16), term

    def forward_documents(tick):
        from_arrivals = lax.dynamic_index_in_dim(
            arrival_docs, jnp.clip(section_pos - tick - 1, 0, section_count - 1), 0, keepdims=False
        )[0]
        step = jnp.clip(tick - section_pos, 0, TICKS - 1)
        from_fresh = fresh_docs[step, plan[step, replica_pos]]
        return jnp.where(section_pos > tick, from_arrivals, from_fresh)

    first_in = balanced[0]
    if section_count > TICKS:
        first_in = jnp.where(section_pos == 0, first_in, shifted(arrivals[0, 0], "section", 1))
    grad_in = jnp.where(
        section_pos == section_count - 1,
        loss_grad[0, 0],
        shifted(returning[0, 0], "section", -1),
    )
    gain_rows = jnp.stack(split_float(gain_row) + [jnp.zeros((width,), BF16)] * 13)
    early = jnp.concatenate([stash[0, 0, 0], stash[1, 0, 0], gain_rows], 0)
    early = lax.all_gather(early, "tensor")
    first_in = tie(first_in, out_x, kv_x)
    firsts = jnp.stack(gather(first_in))

    def early_block(index):
        group = tensor_count // replicas
        block = lax.dynamic_slice_in_dim(early, index * group, group, 0)
        return block.transpose(1, 0, 2).reshape(early.shape[1], block_rows)

    def gain_of(block):
        return sum(block[-16 + i : -15 + i].astype(F32) for i in range(3))

    saved = TICKS * length
    squares = jnp.sum(jnp.square(early[:, :saved].astype(F32)), (0, 2))
    squares = jnp.concatenate([squares, jnp.sum(jnp.square(firsts.astype(F32)), (0, 2))])[:, None]
    rows = []
    for mask in range(replicas):
        block = early_block(replica_pos ^ mask)
        first = lax.dynamic_index_in_dim(firsts, which[mask], 0, keepdims=False)
        row = jnp.concatenate([block[:saved], first], 0).astype(F32) * gain_of(block)
        rows.append(row.astype(BF16))
    gains = [gain_of(early_block(mask ^ shift)) for mask in range(replicas)]
    out_parts = far_dp(w_out[0], out_sibling, out_x)
    kv_parts = far_dp(kv_weight, kv_sibling, kv_x)
    terms = head_terms(grad_in)
    (kv_sum,) = sum_of(fixed(0, 1, 2, 3), rows, [kv_parts])
    query_early = [query_weight[0], query_sibling]
    query_sum = sum_of(fixed(0, 1), rows[:2], [query_early])
    query_x = tie(query_x, kv_sum, *query_sum, *terms)
    query_parts = far_dp(query_weight[0], query_sibling, query_x)
    query_sum = sum_of(fixed(0), rows[2:3], [query_parts[2:3]], (), query_sum)
    query_sum = sum_of(fixed(0), rows[3:], [query_parts[3:]], (), query_sum)
    sums = [*query_sum, kv_sum, squares]
    if bit_count:
        grad_kv_parts = gather_dp(jnp.concatenate(own_kv, 1))
    else:
        grad_kv_parts = kv_parts

    mixed = mix(forward_documents(0), sums, TICKS)
    blocks = gather(mixed)
    going_back, gain_total = backward(
        stash[0, 0, 0], stash_docs[0, 0, 0], grad_in, terms, sums, 0, [mixed]
    )
    outgoing = project_out(first_in, blocks)
    forward_in = jnp.where(section_pos == 0, balanced[1], shifted(outgoing, "section", 1))
    grad_in = jnp.where(
        section_pos == section_count - 1, loss_grad[1, 0], shifted(going_back, "section", -1)
    )
    blocks = gather(forward_in)
    groups = [query_parts, kv_parts]
    terms = head_terms(grad_in, [forward_in])
    later = sum_of(picks(0, 1, 2), blocks[:3], groups, gains[:3])
    later = sum_of(picks(3), blocks[3:], groups, gains[3:], later)
    mixed = mix(forward_documents(1), later, 0)
    blocks = gather(mixed)
    going_back, term = backward(
        stash[1, 0, 0], stash_docs[1, 0, 0], grad_in, terms, sums, 1, [mixed]
    )
    outgoing = project_out(forward_in, blocks)
    gain_total = gain_total + term
    gain_total = gain_total + exchange(gain_total, "dp", 1)
    gain_total = gain_total + exchange(gain_total, "dp", 2)
    gain_grad = gain_total / math.sqrt(TICKS * replicas * length)
    return (outgoing[None, None], going_back[None, None], gain_grad[None])


def solution(mesh):
    return jax.shard_map(
        local,
        mesh=mesh,
        in_specs=(
            P("section", "dp", None, "tensor"),
            P(None, "dp", None, "tensor"),
            P(None, "section", "dp", None, "tensor"),
            P("section", "dp", None, "tensor"),
            P(None, "dp", None, "tensor"),
            P("section", "tensor"),
            P("section", "dp", "tensor"),
            P("section", "dp", "tensor"),
            P("section", "dp", "tensor"),
            P("section", "dp", "tensor"),
            P(),
            P(),
            P(None, "dp", None),
            P(None, "section", "dp", None),
        ),
        out_specs=(
            P("section", "dp", None, "tensor"),
            P("section", "dp", None, "tensor"),
            P("section", "tensor"),
        ),
        check_vma=False,
    )
```

time: 423 us -> 335 us (0.79)
  matrix products: 108 us -> 0 us
  Pallas kernels: 0 us -> 78.8 us
  starting transfers between devices: 84.9 us -> 41.5 us
  local copies, waits for them, and re-layouts: 52.6 us -> 26.1 us
  other arithmetic: 12.3 us -> 24.2 us
  between operations: 9.24 us -> 18.7 us
  waiting for transfers between devices: 153 us -> 144 us
    dot_general x36 -> x0, matrix products: 105 us -> none  [the longest x16 53.2 us: product_scatter(): lax.dot_general(left, rows, contract, preferred_element_type=F32)]
    pallas_call x0 -> x32, Pallas kernels: none -> 78.8 us  [the longest x30 78.8 us: call(): pl.pallas_call(body, grid=(1,), in_specs=[spec if spec is not None else w...]
    ppermute x57 -> x37, starting transfers between devices: 75.5 us -> 35.5 us  [exchange(): return lax.ppermute(block, axis, [(i, i ^ mask) for i in range(count)])]
    dynamic_update_slice x16 -> x0, local copies, waits for them, and re-layouts: 28.4 us -> none  [assemble(): whole = lax.dynamic_update_slice(whole, parts[mask], (row, col))]
    ppermute x57 -> x37, waiting for transfers between devices: 153 us -> 135 us  [exchange(): return lax.ppermute(block, axis, [(i, i ^ mask) for i in range(count)])]
    unnamed x106 -> x138, local copies, waits for them, and re-layouts: 1.58 us -> 11.6 us
    broadcast_in_dim x2 -> x1, local copies, waits for them, and re-layouts: 9.74 us -> 0.11 us  [local(): jnp.concatenate([squares, jnp.sum(jnp.square(firsts.astype(F32)), (0, 2))])]
    ppermute x4 -> x3, waiting for transfers between devices: 0.01 us -> 9.09 us  [shifted(): lax.ppermute(value, axis, [(source, source + steps) for source in range(l...]
  transfers between devices with their start and end apart: 61 -> 41, of which waited for: 22 -> 15; matrix products, arithmetic and copies ran while one was open for 39% -> 11% of each run, Pallas kernels for 0% -> 19%
where the time goes in v2:
time: 335 us; the launch traced here: 333 us
  waiting for transfers between devices  144 us (43%)
  Pallas kernels  78.8 us (24%)
  starting transfers between devices  41.5 us (12%)
  local copies, waits for them, and re-layouts  26.1 us (8%)
  other arithmetic  24.2 us (7%)
  between operations  18.7 us (6%)
    ppermute x37, waiting for transfers between devices, exchange(): return lax.ppermute(block, axis, [(i, i ^ mask) for i in range(count)])  135 us
    pallas_call x30, Pallas kernels, call(): pl.pallas_call(body, grid=(1,), in_specs=[spec if spec is not None else w...  78.8 us
    ppermute x37, starting transfers between devices, exchange(): return lax.ppermute(block, axis, [(i, i ^ mask) for i in range(count)])  35.5 us
    unnamed x138, local copies, waits for them, and re-layouts  11.6 us
    ppermute x3, waiting for transfers between devices, shifted(): lax.ppermute(value, axis, [(source, source + steps) for source in range(l...  9.09 us
  transfers between devices with their start and end apart: 41, of which 15 were waited for; matrix products, arithmetic and copies ran while one was open for 11% of the time, Pallas kernels for 19%

profile of v2, /device:TPU:0, one launch (start us, length us, event | category | flops | bytes accessed | tf_op | source)
XLA Modules:
  0.0 333.0 jit_solution(11684788671470404176)
XLA Ops:
  7.2 3.0 collective-permute-start.2
  21.3 35.7 %collective-permute-done.2.refs_1_.refs_4_.refs_6_ = bf16[1024,1024]{1,0:T(8,128)(2,1)} collective-permute-done((bf16[1024,1024]{1,0:T(8,128)(2,1)}, bf16[1024,1024]{1,0:T(8,128)(2,1)}, u32[]{:S(2)}, u32[]{:S(2)}) %collective-permute-start.2) | collective-permute-done | bytes 2097184 | tf_op jit(solution)/shard_map/ppermute | solution.py:29
  57.5 32.3 %collective-permute-done.1 = bf16[2,128,1024]{2,1,0:T(8,128)(2,1)S(1)} collective-permute-done((bf16[2,128,1024]{2,1,0:T(8,128)(2,1)S(1)}, bf16[2,128,1024]{2,1,0:T(8,128)(2,1)S(1)}, u32[]{:S(2)}, u32[]{:S(2)}) %collective-permute-start.1) | collective-permute-done | bytes 524320 | tf_op jit(solution)/shard_map/ppermute | solution.py:29
  95.7 4.8 %collective-permute-done.11 = bf16[128,1024]{1,0:T(8,128)(2,1)S(1)} collective-permute-done((bf16[128,1024]{1,0:T(8,128)(2,1)}, bf16[128,1024]{1,0:T(8,128)(2,1)S(1)}, u32[]{:S(2)}, u32[]{:S(2)}) %collective-permute-start.11) | collective-permute-done | bytes 262176 | tf_op jit(solution)/shard_map/ppermute | solution.py:35
  104.7 8.8 %collective-permute-done.5 = bf16[128,1024]{1,0:T(8,128)(2,1)} collective-permute-done((bf16[128,1024]{1,0:T(8,128)(2,1)}, bf16[128,1024]{1,0:T(8,128)(2,1)}, u32[]{:S(2)}, u32[]{:S(2)}) %collective-permute-start.5) | collective-permute-done | bytes 262176 | tf_op jit(solution)/shard_map/ppermute | solution.py:29
  115.3 5.5 %collective-permute-done.6 = bf16[128,1024]{1,0:T(8,128)(2,1)} collective-permute-done((bf16[128,1024]{1,0:T(8,128)(2,1)}, bf16[128,1024]{1,0:T(8,128)(2,1)}, u32[]{:S(2)}, u32[]{:S(2)}) %collective-permute-start.6) | collective-permute-done | bytes 262176 | tf_op jit(solution)/shard_map/ppermute | solution.py:29
  130.7 3.8 %shard_map.188 = (bf16[128,1024]{1,0:T(8,128)(2,1)S(1)}, f32[128,1024]{1,0:T(8,128)S(1)}) custom-call(s32[2]{0:T(128)S(1)} %pad_add_fusion.refs_0_, bf16[128,1024]{1,0:T(8,128)(2,1)S(1)} %bitcast_select_fusion.1.refs_1_, bf16[1024,1024]{1,0:T(8,128)(2,1)S(1)} %bitcast.95, bf16[1024,1024]{1,0:T(8,128)(2,1)} %collective-permute-done.12.refs_3_.refs_5_, ...), custom_call_target="tpu_custom_call" | custom-call | flops 1024 | bytes 1024 | tf_op jit(solution)/shard_map/pallas_call | solution.py:50
  134.5 3.1 collective-permute-done.14.refs_1_
  147.2 3.5 %shard_map.185.refs_1_ = f32[384,512]{1,0:T(8,128)S(1)} custom-call(s32[4]{0:T(128)S(1)} %call_exported.0.refs_0_, bf16[384,1024]{1,0:T(8,128)(2,1)S(1)} %get-tuple-element.88.refs_1_, bf16[384,1024]{1,0:T(8,128)(2,1)S(1)} %get-tuple-element.87.refs_2_, bf16[384,1024]{1,0:T(8,128)(2,1)S(1)} %get-tuple-element.86.refs_3_.refs_1_, ...), custom_call_target="tpu_custom_call" | custom-call | flops 1024 | bytes 1024 | tf_op jit(solution)/shard_map/pallas_call | solution.py:50
  180.0 5.0 %shard_map.204 = (bf16[128,1024]{1,0:T(8,128)(2,1)}, f32[128,1024]{1,0:T(8,128)S(1)}) custom-call(s32[2]{0:T(128)S(1)} %copy-done.38, bf16[128,1024]{1,0:T(8,128)(2,1)S(1)} %get-tuple-element.31.refs_1_, bf16[128,512]{1,0:T(8,128)(2,1)S(1)} %get-tuple-element.32.refs_2_, bf16[1024,1024]{1,0:T(8,128)(2,1)S(1)} %bitcast.108, ...), custom_call_target="tpu_custom_call" | custom-call | flops 1024 | bytes 1024 | tf_op jit(solution)/shard_map/pallas_call | solution.py:50
  185.0 9.1 %collective-permute-done.18.refs_3_ = bf16[128,1024]{1,0:T(8,128)(2,1)} collective-permute-done((bf16[128,1024]{1,0:T(8,128)(2,1)}, bf16[128,1024]{1,0:T(8,128)(2,1)}, u32[]{:S(2)}, u32[]{:S(2)}) %collective-permute-start.18) | collective-permute-done | bytes 262176 | tf_op jit(solution)/shard_map/ppermute | solution.py:29
  202.8 3.8 %shard_map.195.refs_6_ = f32[128,1024]{1,0:T(8,128)S(1)} custom-call(s32[3]{0:T(128)S(1)} %copy-done.41, bf16[128,1024]{1,0:T(8,128)(2,1)} %shard_map.194.refs_1_.refs_8_, bf16[128,1024]{1,0:T(8,128)(2,1)} %collective-permute-done.20.refs_2_, bf16[128,1024]{1,0:T(8,128)(2,1)} %collective-permute-done.18.refs_3_, bf16[1024,1024]{1,0:T(8,128)(2,1)S(1)} %bitcast.97, ...), custom_call_target="tpu_custom_call" | custom-call | flops 1024 | bytes 1024 | tf_op jit(solution)/shard_map/pallas_call | solution.py:50
  209.3 3.5 %shard_map.196 = bf16[128,1024]{1,0:T(8,128)(2,1)} custom-call(s32[1]{0:T(128)} %bitcast.refs_0_, bf16[128,1024]{1,0:T(8,128)(2,1)} %collective-permute-done.19.refs_1_, bf16[1024,1024]{1,0:T(8,128)(2,1)S(1)} %bitcast.98, bf16[1024,1024]{1,0:T(8,128)(2,1)} %collective-permute-done.12.refs_3_.refs_5_, ...), custom_call_target="tpu_custom_call" | custom-call | flops 1024 | bytes 1024 | tf_op jit(solution)/shard_map/pallas_call | solution.py:50
  212.8 3.4 %collective-permute-start.21 = (bf16[128,1024]{1,0:T(8,128)(2,1)}, bf16[128,1024]{1,0:T(8,128)(2,1)}, u32[]{:S(2)}, u32[]{:S(2)}) collective-permute-start(bf16[128,1024]{1,0:T(8,128)(2,1)} %shard_map.196), channel_id=1, source_target_pairs={{0,4},{1,5},{2,6},{3,7},{8,12},{9,13},{10,14},{11,15},{16,20},{17,... | collective-permute-start | bytes 786440 | tf_op jit(solution)/shard_map/ppermute | solution.py:35
  223.7 4.3 %collective-permute-done.31 = bf16[128,1024]{1,0:T(8,128)(2,1)} collective-permute-done((bf16[128,1024]{1,0:T(8,128)(2,1)}, bf16[128,1024]{1,0:T(8,128)(2,1)}, u32[]{:S(2)}, u32[]{:S(2)}) %collective-permute-start.31) | collective-permute-done | bytes 262176 | tf_op jit(solution)/shard_map/ppermute | solution.py:35
  235.3 4.2 %shard_map.208 = (bf16[128,1024]{1,0:T(8,128)(2,1)}, f32[128,1024]{1,0:T(8,128)S(1)}) custom-call(s32[2]{0:T(128)S(1)} %copy-done.39, bf16[128,1024]{1,0:T(8,128)(2,1)S(1)} %bitcast_select_fusion.refs_1_, bf16[1024,1024]{1,0:T(8,128)(2,1)S(1)} %bitcast.100, bf16[1024,1024]{1,0:T(8,128)(2,1)} %collective-permute-done.12.refs_3_.refs_5_, ...), custom_call_target="tpu_custom_call" | custom-call | flops 1024 | bytes 1024 | tf_op jit(solution)/shard_map/pallas_call | solution.py:50
  243.5 8.7 %collective-permute-done.24.refs_2_ = bf16[128,1024]{1,0:T(8,128)(2,1)} collective-permute-done((bf16[128,1024]{1,0:T(8,128)(2,1)}, bf16[128,1024]{1,0:T(8,128)(2,1)}, u32[]{:S(2)}, u32[]{:S(2)}) %collective-permute-start.24) | collective-permute-done | bytes 262176 | tf_op jit(solution)/shard_map/ppermute | solution.py:29
  253.8 4.7 %shard_map.197 = (f32[128,1024]{1,0:T(8,128)S(1)}, f32[128,512]{1,0:T(8,128)S(1)}, f32[128,1]{1,0:T(8,128)S(1)}) custom-call(s32[3]{0:T(128)S(1)} %copy-done.42, bf16[128,1024]{1,0:T(8,128)(2,1)} %fusion.9.refs_1_.refs_7_.refs_6_, bf16[128,1024]{1,0:T(8,128)(2,1)} %collective-permute-done.24.refs_2_, bf16[128,1024]{1,0:T(8,128)(2,1)} %collective-permute-done.22.refs_3_, ...), custom_call_target="tpu_custom_call" | custom-call | flops 1024 | bytes 1024 | tf_op jit(solution)/shard_map/pallas_call | solution.py:50
  260.1 3.4 %shard_map.198 = (f32[128,1024]{1,0:T(8,128)S(1)}, f32[128,512]{1,0:T(8,128)S(1)}, f32[128,1]{1,0:T(8,128)S(1)}) custom-call(s32[1]{0:T(128)} %bitcast.refs_0_, bf16[128,1024]{1,0:T(8,128)(2,1)} %collective-permute-done.23.refs_1_, f32[1,1024]{1,0:T(1,128)S(1)} %get-tuple-element.57.refs_2_, bf16[1024,1024]{1,0:T(8,128)(2,1)S(1)} %bitcast.111, ...), custom_call_target="tpu_custom_call" | custom-call | flops 1024 | bytes 1024 | tf_op jit(solution)/shard_map/pallas_call | solution.py:50
  270.9 5.0 %shard_map.213 = (bf16[128,1024]{1,0:T(8,128)(2,1)}, f32[128,1024]{1,0:T(8,128)S(1)}) custom-call(s32[2]{0:T(128)S(1)} %copy-done.40, bf16[128,1024]{1,0:T(8,128)(2,1)S(1)} %get-tuple-element.38.refs_1_, bf16[128,512]{1,0:T(8,128)(2,1)S(1)} %get-tuple-element.39.refs_2_, bf16[1024,1024]{1,0:T(8,128)(2,1)S(1)} %bitcast.113, ...), custom_call_target="tpu_custom_call" | custom-call | flops 1024 | bytes 1024 | tf_op jit(solution)/shard_map/pallas_call | solution.py:50
  276.0 4.2 %collective-permute-done.35.refs_1_ = bf16[128,1152]{1,0:T(8,128)(2,1)S(1)} collective-permute-done((bf16[128,1152]{1,0:T(8,128)(2,1)S(1)}, bf16[128,1152]{1,0:T(8,128)(2,1)S(1)}, u32[]{:S(2)}, u32[]{:S(2)}) %collective-permute-start.35) | collective-permute-done | bytes 294944 | tf_op jit(solution)/shard_map/ppermute | solution.py:29
  287.5 20.9 %collective-permute-done.25.refs_3_ = bf16[128,1024]{1,0:T(8,128)(2,1)} collective-permute-done((bf16[128,1024]{1,0:T(8,128)(2,1)}, bf16[128,1024]{1,0:T(8,128)(2,1)}, u32[]{:S(2)}, u32[]{:S(2)}) %collective-permute-start.25) | collective-permute-done | bytes 262176 | tf_op jit(solution)/shard_map/ppermute | solution.py:29
  318.2 3.8 %shard_map.200.refs_6_ = f32[128,1024]{1,0:T(8,128)S(1)} custom-call(s32[3]{0:T(128)S(1)} %copy-done.43, bf16[128,1024]{1,0:T(8,128)(2,1)} %shard_map.199.refs_1_.refs_8_, bf16[128,1024]{1,0:T(8,128)(2,1)S(1)} %collective-permute-done.27.refs_2_, bf16[128,1024]{1,0:T(8,128)(2,1)} %collective-permute-done.25.refs_3_, bf16[1024,1024]{1,0:T(8,128)(2,1)S(1)} %bitcast.102, ...), custom_call_target="tpu_custom_call" | custom-call | flops 1024 | bytes 1024 | tf_op jit(solution)/shard_map/pallas_call | solution.py:50
  322.0 3.5 %shard_map.201 = bf16[128,1024]{1,0:T(8,128)(2,1)} custom-call(s32[1]{0:T(128)} %bitcast.refs_0_, bf16[128,1024]{1,0:T(8,128)(2,1)S(1)} %collective-permute-done.26.refs_1_, bf16[1024,1024]{1,0:T(8,128)(2,1)S(1)} %bitcast.103, bf16[1024,1024]{1,0:T(8,128)(2,1)} %collective-permute-done.12.refs_3_.refs_5_, ...), custom_call_target="tpu_custom_call" | custom-call | flops 1024 | bytes 1024 | tf_op jit(solution)/shard_map/pallas_call | solution.py:50
  (275 shorter events, 126.2 us)
Async XLA Ops:
  7.2 116.2 %all-gather.3.cloned.1.call-start = ((), (), s32[]{:S(2)}) async-start(), calls=%async_computation | async-start | bytes 2785280 | tf_op jit(solution)/shard_map/all_gather | solution.py:516
  7.2 49.8 %collective-permute-start.2 = (bf16[1024,1024]{1,0:T(8,128)(2,1)}, bf16[1024,1024]{1,0:T(8,128)(2,1)}, u32[]{:S(2)}, u32[]{:S(2)}) collective-permute-start(bf16[1024,1024]{1,0:T(8,128)(2,1)} %bitcast.92), channel_id=1, source_target_pairs={{0,16},{8,24},{16,0},{24,8},{1,17},{9,25},{17,1},{25,9},{2,18},{10... | collective-permute-start | bytes 6291464 | tf_op jit(solution)/shard_map/ppermute | solution.py:29
  14.8 88.3 %collective-permute-start.12 = (bf16[1024,1024]{1,0:T(8,128)(2,1)S(1)}, bf16[1024,1024]{1,0:T(8,128)(2,1)}, u32[]{:S(2)}, u32[]{:S(2)}) collective-permute-start(bf16[1024,1024]{1,0:T(8,128)(2,1)S(1)} %bitcast.93), channel_id=1, source_target_pairs={{0,8},{8,0},{16,24},{24,16},{1,9},{9,1},{17,25},{25,17},{2,10},{10... | collective-permute-start | bytes 6291464 | tf_op jit(solution)/shard_map/ppermute | solution.py:29
  16.7 74.8 %collective-permute-start.3 = (bf16[1024,512]{1,0:T(8,128)(2,1)S(1)}, bf16[1024,512]{1,0:T(8,128)(2,1)}, u32[]{:S(2)}, u32[]{:S(2)}) collective-permute-start(bf16[1024,512]{1,0:T(8,128)(2,1)S(1)} %pad_maximum_fusion.refs_5_.refs_11_.refs_7_), channel_id=1, source_target_pairs={{0,16},{8,24},{16,0},{24,8},{1,17},{9,25},{17,1},{25,9},{2,18},{10... | collective-permute-start | bytes 3145736 | tf_op jit(solution)/shard_map/ppermute | solution.py:29
  21.1 68.7 %collective-permute-start.1 = (bf16[2,128,1024]{2,1,0:T(8,128)(2,1)S(1)}, bf16[2,128,1024]{2,1,0:T(8,128)(2,1)S(1)}, u32[]{:S(2)}, u32[]{:S(2)}) collective-permute-start(bf16[2,128,1024]{2,1,0:T(8,128)(2,1)S(1)} %broadcast_select_fusion), channel_id=1, source_target_pairs={{0,16},{8,24},{16,0},{24,8},{1,17},{9,25},{17,1},{25,9},{2,18},{10... | collective-permute-start | bytes 1572872 | tf_op jit(solution)/shard_map/ppermute | solution.py:29
  57.0 69.4 %collective-permute-start.13 = (bf16[1024,1024]{1,0:T(8,128)(2,1)}, bf16[1024,1024]{1,0:T(8,128)(2,1)}, u32[]{:S(2)}, u32[]{:S(2)}) collective-permute-start(bf16[1024,1024]{1,0:T(8,128)(2,1)} %collective-permute-done.2.refs_1_.refs_4_.refs_6_), channel_id=1, source_target_pairs={{0,8},{8,0},{16,24},{24,16},{1,9},{9,1},{17,25},{25,17},{2,10},{10... | collective-permute-start | bytes 6291464 | tf_op jit(solution)/shard_map/ppermute | solution.py:29
  57.0 82.0 %collective-permute-start.10 = (bf16[1024,1024]{1,0:T(8,128)(2,1)}, bf16[1024,1024]{1,0:T(8,128)(2,1)}, u32[]{:S(2)}, u32[]{:S(2)}) collective-permute-start(bf16[1024,1024]{1,0:T(8,128)(2,1)} %bitcast.104), channel_id=1, source_target_pairs={{0,8},{8,0},{16,24},{24,16},{1,9},{9,1},{17,25},{25,17},{2,10},{10... | collective-permute-start | bytes 6291464 | tf_op jit(solution)/shard_map/ppermute | solution.py:29
  89.8 63.9 %collective-permute-start.7 = (bf16[1024,1024]{1,0:T(8,128)(2,1)}, bf16[1024,1024]{1,0:T(8,128)(2,1)}, u32[]{:S(2)}, u32[]{:S(2)}) collective-permute-start(bf16[1024,1024]{1,0:T(8,128)(2,1)} %bitcast.105), channel_id=1, source_target_pairs={{0,16},{8,24},{16,0},{24,8},{1,17},{9,25},{17,1},{25,9},{2,18},{10... | collective-permute-start | bytes 6291464 | tf_op jit(solution)/shard_map/ppermute | solution.py:29
  115.3 31.9 %collective-permute-start.8 = (bf16[1024,512]{1,0:T(8,128)(2,1)S(1)}, bf16[1024,512]{1,0:T(8,128)(2,1)}, u32[]{:S(2)}, u32[]{:S(2)}) collective-permute-start(bf16[1024,512]{1,0:T(8,128)(2,1)S(1)} %pad_maximum_fusion.refs_5_.refs_11_.refs_7_), channel_id=1, source_target_pairs={{0,8},{8,0},{16,24},{24,16},{1,9},{9,1},{17,25},{25,17},{2,10},{10... | collective-permute-start | bytes 3145736 | tf_op jit(solution)/shard_map/ppermute | solution.py:29
  120.9 26.3 %collective-permute-start.9 = (bf16[1024,512]{1,0:T(8,128)(2,1)}, bf16[1024,512]{1,0:T(8,128)(2,1)}, u32[]{:S(2)}, u32[]{:S(2)}) collective-permute-start(bf16[1024,512]{1,0:T(8,128)(2,1)} %collective-permute-done.3.refs_2_.refs_7_.refs_13_.refs_9_), channel_id=1, source_target_pairs={{0,8},{8,0},{16,24},{24,16},{1,9},{9,1},{17,25},{25,17},{2,10},{10... | collective-permute-start | bytes 3145736 | tf_op jit(solution)/shard_map/ppermute | solution.py:29
  137.6 16.1 %collective-permute-start.15 = (bf16[128,1024]{1,0:T(8,128)(2,1)S(1)}, bf16[128,1024]{1,0:T(8,128)(2,1)}, u32[]{:S(2)}, u32[]{:S(2)}) collective-permute-start(bf16[128,1024]{1,0:T(8,128)(2,1)S(1)} %get-tuple-element.24), channel_id=1, source_target_pairs={{0,1},{1,0},{2,3},{3,2},{4,5},{5,4},{6,7},{7,6},{8,9},{9,8},{10,11... | collective-permute-start | bytes 786440 | tf_op jit(solution)/shard_map/ppermute | solution.py:29
  176.9 17.2 %collective-permute-start.28 = (bf16[128,1152]{1,0:T(8,128)(2,1)S(1)}, bf16[128,1152]{1,0:T(8,128)(2,1)S(1)}, u32[]{:S(2)}, u32[]{:S(2)}) collective-permute-start(bf16[128,1152]{1,0:T(8,128)(2,1)S(1)} %shard_map.203.refs_11_), channel_id=1, source_target_pairs={{0,1},{1,0},{2,3},{3,2},{4,5},{5,4},{6,7},{7,6},{8,9},{9,8},{10,11... | collective-permute-start | bytes 884744 | tf_op jit(solution)/shard_map/ppermute | solution.py:29
  178.7 15.4 %collective-permute-start.18 = (bf16[128,1024]{1,0:T(8,128)(2,1)}, bf16[128,1024]{1,0:T(8,128)(2,1)}, u32[]{:S(2)}, u32[]{:S(2)}) collective-permute-start(bf16[128,1024]{1,0:T(8,128)(2,1)} %shard_map.194.refs_1_.refs_8_), channel_id=1, source_target_pairs={{0,2},{1,3},{2,0},{3,1},{4,6},{5,7},{6,4},{7,5},{8,10},{9,11},{10,... | collective-permute-start | bytes 786440 | tf_op jit(solution)/shard_map/ppermute | solution.py:29
  178.7 23.3 %collective-permute-start.20 = (bf16[128,1024]{1,0:T(8,128)(2,1)}, bf16[128,1024]{1,0:T(8,128)(2,1)}, u32[]{:S(2)}, u32[]{:S(2)}) collective-permute-start(bf16[128,1024]{1,0:T(8,128)(2,1)} %shard_map.194.refs_1_.refs_8_), channel_id=1, source_target_pairs={{0,1},{1,0},{2,3},{3,2},{4,5},{5,4},{6,7},{7,6},{8,9},{9,8},{10,11... | collective-permute-start | bytes 786440 | tf_op jit(solution)/shard_map/ppermute | solution.py:29
  195.0 21.3 %collective-permute-start.30 = (bf16[128,1152]{1,0:T(8,128)(2,1)}, bf16[128,1152]{1,0:T(8,128)(2,1)}, u32[]{:S(2)}, u32[]{:S(2)}) collective-permute-start(bf16[128,1152]{1,0:T(8,128)(2,1)} %shard_map.205.refs_11_), channel_id=1, source_target_pairs={{0,2},{1,3},{2,0},{3,1},{4,6},{5,7},{6,4},{7,5},{8,10},{9,11},{10,... | collective-permute-start | bytes 884744 | tf_op jit(solution)/shard_map/ppermute | solution.py:29
  196.6 20.7 %collective-permute-start.29 = (bf16[128,1024]{1,0:T(8,128)(2,1)}, bf16[128,1024]{1,0:T(8,128)(2,1)}, u32[]{:S(2)}, u32[]{:S(2)}) collective-permute-start(bf16[128,1024]{1,0:T(8,128)(2,1)} %get-tuple-element.35), channel_id=1, source_target_pairs={{0,1},{1,0},{2,3},{3,2},{4,5},{5,4},{6,7},{7,6},{8,9},{9,8},{10,11... | collective-permute-start | bytes 786440 | tf_op jit(solution)/shard_map/ppermute | solution.py:29
  232.5 19.7 %collective-permute-start.24 = (bf16[128,1024]{1,0:T(8,128)(2,1)}, bf16[128,1024]{1,0:T(8,128)(2,1)}, u32[]{:S(2)}, u32[]{:S(2)}) collective-permute-start(bf16[128,1024]{1,0:T(8,128)(2,1)} %fusion.9.refs_1_.refs_7_.refs_6_), channel_id=1, source_target_pairs={{0,1},{1,0},{2,3},{3,2},{4,5},{5,4},{6,7},{7,6},{8,9},{9,8},{10,11... | collective-permute-start | bytes 786440 | tf_op jit(solution)/shard_map/ppermute | solution.py:29
  235.3 24.3 %collective-permute-start.23 = (bf16[128,1024]{1,0:T(8,128)(2,1)}, bf16[128,1024]{1,0:T(8,128)(2,1)}, u32[]{:S(2)}, u32[]{:S(2)}) collective-permute-start(bf16[128,1024]{1,0:T(8,128)(2,1)} %collective-permute-done.22.refs_3_), channel_id=1, source_target_pairs={{0,1},{1,0},{2,3},{3,2},{4,5},{5,4},{6,7},{7,6},{8,9},{9,8},{10,11... | collective-permute-start | bytes 786440 | tf_op jit(solution)/shard_map/ppermute | solution.py:29
  239.6 25.5 %collective-permute-start.33 = (bf16[128,1024]{1,0:T(8,128)(2,1)}, bf16[128,1024]{1,0:T(8,128)(2,1)}, u32[]{:S(2)}, u32[]{:S(2)}) collective-permute-start(bf16[128,1024]{1,0:T(8,128)(2,1)} %get-tuple-element.37), channel_id=1, source_target_pairs={{0,1},{1,0},{2,3},{3,2},{4,5},{5,4},{6,7},{7,6},{8,9},{9,8},{10,11... | collective-permute-start | bytes 786440 | tf_op jit(solution)/shard_map/ppermute | solution.py:29
  241.6 23.4 %collective-permute-start.34 = (bf16[128,1024]{1,0:T(8,128)(2,1)}, bf16[128,1024]{1,0:T(8,128)(2,1)}, u32[]{:S(2)}, u32[]{:S(2)}) collective-permute-start(bf16[128,1024]{1,0:T(8,128)(2,1)} %shard_map.209.refs_6_), channel_id=1, source_target_pairs={{0,2},{1,3},{2,0},{3,1},{4,6},{5,7},{6,4},{7,5},{8,10},{9,11},{10,... | collective-permute-start | bytes 786440 | tf_op jit(solution)/shard_map/ppermute | solution.py:29
  281.1 31.7 %collective-permute-start.37 = (bf16[128,1152]{1,0:T(8,128)(2,1)}, bf16[128,1152]{1,0:T(8,128)(2,1)}, u32[]{:S(2)}, u32[]{:S(2)}) collective-permute-start(bf16[128,1152]{1,0:T(8,128)(2,1)} %shard_map.214.refs_11_), channel_id=1, source_target_pairs={{0,2},{1,3},{2,0},{3,1},{4,6},{5,7},{6,4},{7,5},{8,10},{9,11},{10,... | collective-permute-start | bytes 884744 | tf_op jit(solution)/shard_map/ppermute | solution.py:29
  281.9 26.6 %collective-permute-start.25 = (bf16[128,1024]{1,0:T(8,128)(2,1)}, bf16[128,1024]{1,0:T(8,128)(2,1)}, u32[]{:S(2)}, u32[]{:S(2)}) collective-permute-start(bf16[128,1024]{1,0:T(8,128)(2,1)} %shard_map.199.refs_1_.refs_8_), channel_id=1, source_target_pairs={{0,2},{1,3},{2,0},{3,1},{4,6},{5,7},{6,4},{7,5},{8,10},{9,11},{10,... | collective-permute-start | bytes 786440 | tf_op jit(solution)/shard_map/ppermute | solution.py:29
  284.1 29.8 %collective-permute-start.36 = (bf16[128,1024]{1,0:T(8,128)(2,1)}, bf16[128,1024]{1,0:T(8,128)(2,1)}, u32[]{:S(2)}, u32[]{:S(2)}) collective-permute-start(bf16[128,1024]{1,0:T(8,128)(2,1)} %get-tuple-element.42), channel_id=1, source_target_pairs={{0,1},{1,0},{2,3},{3,2},{4,5},{5,4},{6,7},{7,6},{8,9},{9,8},{10,11... | collective-permute-start | bytes 786440 | tf_op jit(solution)/shard_map/ppermute | solution.py:29
  285.8 32.4 %collective-permute-start.27 = (bf16[128,1024]{1,0:T(8,128)(2,1)}, bf16[128,1024]{1,0:T(8,128)(2,1)S(1)}, u32[]{:S(2)}, u32[]{:S(2)}) collective-permute-start(bf16[128,1024]{1,0:T(8,128)(2,1)} %shard_map.199.refs_1_.refs_8_), channel_id=1, source_target_pairs={{0,1},{1,0},{2,3},{3,2},{4,5},{5,4},{6,7},{7,6},{8,9},{9,8},{10,11... | collective-permute-start | bytes 786440 | tf_op jit(solution)/shard_map/ppermute | solution.py:29
  (86 other events, 609.7 us)
Sparse Core Ops, SparseCore 0:
  14.9 48.6 all-gather.2
